TPU v7x, 128 devices: a whole 4x4x4 slice. The times are simulated.
128 devices in a mesh: gx: 32 (over y, z_lo, x), gy: 4 (over z_hi, core).
Axes of the slice: x: 4, y: 4, z: 4 (z_hi: 2, z_lo: 2; z = z_hi * 2 + z_lo), core: 2. Of those that a mesh axis runs over, the one named last changes fastest.
Arguments:
- noisy: float32 [16, 512, 512], P(None, 'gx', 'gy'), may hold values from -6 to 6
- strength: float32 [16], replicated, may hold values from 0.5 to 4
Outputs:
- denoised: float32 [16, 512, 512], P(None, 'gx', 'gy')
All inputs are finite; a program needn't handle non-finite values.
Results may differ from a plain program's by a relative error of at most 0.00002.
Values sent between devices are 32-bit elements; how exact they have to be, the bound alone decides.
No kernel may reach another device: no remote copies, remote signals or barrier semaphores. Data moves between devices by JAX's collectives and lax.ppermute only.
A program may use at most 128 MiB of HBM per device.

v0:
```python
import math

import jax
import jax.numpy as jnp
from jax import lax
from jax.experimental import pallas as pl
from jax.experimental.pallas import tpu as pltpu
from jax.sharding import PartitionSpec as P

F = jnp.float32
B = jnp.bfloat16
HALO = 4


def lanes():
    return lax.broadcasted_iota(jnp.int32, (8, 128), 1)


def lane_roll(value, steps):
    steps %= 128
    return pltpu.roll(value, steps, 1) if steps else value


def offsets(shift_z, sy):
    if shift_z:
        return (-2, -1, 0, 1, 2)
    return (0, 1, 2) if sy > 2 else (1, 2)


def moved_row(copies, sy, row, shift_z, parity):
    k = shift_z + parity
    return copies[sy, row, k % 2, k // 2 : k // 2 + 8]


def fill_copies(copies, count, row):
    flat = copies.reshape(5 * count * 2 * 16, 128)
    for slot in range(0, 10 * count, 8):
        flat[pl.ds(16 * slot + 8, 8, stride=16)] = jnp.zeros((8, 128), F)
    for x in range(count):
        for parity in range(2):
            value = row(x, parity)
            for sy in range(5):
                copies[sy, x, parity, 0:8] = lane_roll(value, 2 - sy)


def fill_below(below, squares, blocks):
    count = below.shape[1]
    for sy in range(5):
        for x in range(count):
            for j in range(3):
                below[sy, x, j] = jnp.zeros((8, 128), F)
    flat = below.reshape(5 * count * 3 * 8, 128)
    for source, target, many in blocks:
        sums = []
        for parity in range(2):
            total = squares[parity, source : source + many]
            for step in range(1, 5):
                total = total + squares[parity, source + step : source + step + many]
            near = lane_roll(total, 1) + lane_roll(total, 127)
            far = lane_roll(total, 2) + lane_roll(total, 126)
            sums.append(total + near + far)
        three = (sums[0], sums[0] + sums[1], sums[1])
        for j in range(3):
            for sy in range(5):
                flat[pl.ds(((sy * count + target) * 3 + j) * 8, many, stride=24)] = lane_roll(three[j], 2 - sy)


def put_squares(squares, at, ref, count):
    flat = ref.reshape(count * 16, 128)
    for parity in range(2):
        for start in range(0, count, 8):
            many = min(8, count - start)
            value = flat[pl.ds(parity * 8 + 16 * start, many, stride=16)]
            squares[parity, at + start : at + start + many] = value * value


def clear_sides(sides):
    slots = sides.shape[0] * sides.shape[1] * 3
    flat = sides.reshape(slots * 24, 128)
    for slot in range(0, slots, 8):
        flat[pl.ds(24 * slot + 7, 8, stride=24)] = jnp.zeros((8, 128), F)
        flat[pl.ds(24 * slot + 16, 8, stride=24)] = jnp.zeros((8, 128), F)


def patch_sums(rows, row, moved, sides, parts, base):
    first, count = rows
    squared, pairs, fours = {}, {}, {}

    def square(m):
        if m not in squared:
            x = first - 2 + m
            differences = [row(x, parity) - moved(x, parity) for parity in range(2)]
            squared[m] = [d * d for d in differences]
        return squared[m]

    def pair(m):
        if m not in pairs:
            pairs[m] = [a + b for a, b in zip(square(m), square(m + 1))]
        return pairs[m]

    def four(m):
        if m not in fours:
            fours[m] = [a + b for a, b in zip(pair(m), pair(m + 2))]
        return fours[m]

    for j in range(count):
        shared, other = (four(j + 1), square(j)) if j % 2 == 0 else (four(j), square(j + 4))
        even, odd = [a + b for a, b in zip(shared, other)]
        both = even + odd
        sides[j, 0, 8:16] = both
        sides[j, 1, 8:16] = even
        sides[j, 2, 8:16] = odd
        even = both + sides[j, 0, 7:15] + sides[j, 1, 9:17]
        odd = both + sides[j, 0, 9:17] + sides[j, 2, 7:15]
        sums = jnp.concatenate([even, odd], 0)
        high = sums.astype(B)
        at = base + 16 * j
        parts[at : at + 16, 0:128] = high
        parts[at : at + 16, 128:256] = (sums - high.astype(F)).astype(B)


def accumulate(nx, segments, row, moved, below, rates, masks, column_mask, start, scratch):
    sides, parts, kept, carry, weighted, totals = scratch
    last_slice = lax.broadcasted_iota(jnp.int32, (8, 128), 0) == 7
    clear_sides(sides)
    carry_flat = carry.reshape(2 * nx * 4 * 16, 128)
    for slot in range(0, 8 * nx, 8):
        carry_flat[pl.ds(16 * slot + 7, 8, stride=16)] = jnp.zeros((8, 128), F)
    for x in range(nx):
        for parity in range(2):
            weighted[x, parity], totals[x, parity] = start(x, parity)
    line = lax.broadcasted_iota(jnp.int32, (256, 128), 0) % 128
    column = lax.broadcasted_iota(jnp.int32, (256, 128), 1)
    band = jnp.where(abs(line - column) <= 2, 1.0, 0.0).astype(B)
    for sy in range(5):
        place = {}
        for shift_z in range(3):
            base, todo = 0, []
            for n, shift_x in enumerate(offsets(shift_z, sy)):
                slot = 0
                for rows in segments(shift_x):
                    patch_sums(
                        rows,
                        row,
                        lambda x, parity: moved(sy, x + shift_x, shift_z, parity),
                        sides.at[n, slot : slot + rows[1]],
                        parts,
                        base,
                    )
                    todo.append((shift_x, rows, base, n, slot))
                    base += 16 * rows[1]
                    slot += rows[1]
            sums = jnp.dot(parts[0:base], band, preferred_element_type=F)
            for shift_x, rows, at, n, slot in todo:
                for j in range(rows[1]):
                    x = rows[0] + j
                    for parity in range(2):
                        distance = sums[at + 16 * j + 8 * parity : at + 16 * j + 8 * parity + 8]
                        if shift_z:
                            distance = distance + below(sy, x + shift_x, (shift_z - 1) * (1 + parity))
                        weight = jnp.exp2(distance * rates[parity])
                        if x < 0 or x + shift_x < 0:
                            weight = weight * masks[0]
                        if x >= nx or x + shift_x >= nx:
                            weight = weight * masks[1]
                        if column_mask is not None:
                            weight = weight * column_mask[sy]
                        spot = (sy % 2, shift_z * 5 + n, slot + j, parity)
                        kept[spot] = weight
                        place[shift_z, shift_x, x, parity] = spot
        for x in range(nx):
            gather(sy, x, place, row, moved, kept, carry.at[sy % 2, x], last_slice, weighted, totals)


def plus(a, b):
    return b if a is None else a if b is None else a + b


def gather(sy, x, place, row, moved, kept, carry, last_slice, weighted, totals):
    ahead = [[None, None], [None, None]]
    back = [[[None, None] for _ in range(3)] for _ in range(2)]
    for shift_z in range(3):
        count = [None, None]
        for shift_x in offsets(shift_z, sy):
            for parity in range(2):
                spot = place.get((shift_z, shift_x, x, parity))
                if spot is not None:
                    weight = kept[spot]
                    ahead[0][parity] = plus(ahead[0][parity], weight * moved(sy, x + shift_x, shift_z, parity))
                    count[parity] = plus(count[parity], weight)
                spot = place.get((shift_z, shift_x, x - shift_x, parity))
                if spot is not None:
                    weight = kept[spot]
                    back[0][shift_z][parity] = plus(back[0][shift_z][parity], weight * row(x - shift_x, parity))
                    back[1][shift_z][parity] = plus(back[1][shift_z][parity], weight)
        for parity in range(2):
            if shift_z + parity >= 2 and count[parity] is not None:
                count[parity] = jnp.where(last_slice, 0.0, count[parity])
            ahead[1][parity] = plus(ahead[1][parity], count[parity])
    for m, total in enumerate((weighted, totals)):
        here = [plus(back[m][0][0], None), plus(back[m][0][1], back[m][1][0])]
        for parity, up in enumerate((plus(back[m][1][1], back[m][2][0]), back[m][2][1])):
            if up is not None:
                carry[2 * m + parity, 8:16] = up
                here[parity] = plus(here[parity], carry[2 * m + parity, 7:15])
        for parity in range(2):
            term = ahead[m][parity]
            if here[parity] is not None:
                term = plus(term, lane_roll(here[parity], sy - 2))
            if term is not None:
                total[x, parity] = total[x, parity] + term


def work(nx, rows):
    return [
        pltpu.VMEM((5, rows, 3, 24, 128), F),
        pltpu.VMEM((5 * 16 * rows, 256), B),
        pltpu.VMEM((2, 15, rows, 2, 8, 128), F),
        pltpu.VMEM((2, nx, 4, 16, 128), F),
    ]


def pack_kernel(strength_ref, noisy_ref, own_ref, first_ref, last_ref, rate_ref):
    flat = noisy_ref.reshape(256, 128)
    for x in range(16):
        for parity in range(2):
            value = flat[pl.ds(parity * 16 + x, 8, stride=32)]
            own_ref[x, parity] = value
            if x < HALO:
                first_ref[x, parity] = value
            if x >= 16 - HALO:
                last_ref[x - 16 + HALO, parity] = value
    sublane = lax.broadcasted_iota(jnp.int32, (8, 128), 0)
    for parity in range(2):
        strength = jnp.full((8, 128), 1.0, F)
        for s in range(8):
            strength = jnp.where(sublane == s, strength_ref[2 * s + parity], strength)
        rate_ref[parity] = (-math.log2(math.e) / 125.0) / strength


def inner_segments(shift_x):
    return ((2 + max(0, -shift_x), 12 - abs(shift_x)),)


def outer_segments(shift_x):
    many = 2 + abs(shift_x)
    return ((-max(0, shift_x), many), (14 - max(0, shift_x), many))


def whole_segments(nx):
    return lambda shift_x: ((-max(0, shift_x), nx + abs(shift_x)),)


def to_strips(value, chunk):
    lane = lanes() - 32 * chunk
    right = jnp.where((lane >= 16) & (lane < 24), lane_roll(value, 24 + 32 * chunk), 0.0)
    return jnp.where((lane >= 4) & (lane < 12), lane_roll(value, 4 + 32 * chunk), right)


def inner_kernel(own_ref, rate_ref, copies, weighted, totals, rim_ref, left_ref, right_ref, below, squares, *scratch):
    def row(x, parity):
        return own_ref[x, parity]

    fill_copies(copies, 16, row)
    put_squares(squares, 0, own_ref, 16)
    fill_below(below, squares, ((0, 0, 8), (8, 8, 4)))
    lane = lanes()
    place = (lane % 32) // 4
    for x in range(12):
        for parity in range(2):
            value = jnp.zeros((8, 128), F)
            for chunk in range(4):
                source = 4 * chunk + x - HALO
                if 0 <= source < 16:
                    value = value + to_strips(own_ref[source, parity], chunk)
            rim_ref[x, parity] = value
    for group in range(3):
        for ref, column in ((left_ref, 0), (right_ref, 124)):
            message = jnp.zeros((8, 128), F)
            for chunk in range(4):
                for slot in range(8):
                    source = 4 * chunk + 4 * group + slot // 2 - HALO
                    if 0 <= source < 16:
                        here = (place == slot) & (lane // 32 == chunk)
                        message = jnp.where(here, lane_roll(own_ref[source, slot % 2], 32 * chunk + 4 * slot - column), message)
            ref[group] = message
    one = jnp.ones((8, 128), F)
    accumulate(
        16,
        inner_segments,
        row,
        lambda sy, x, shift_z, parity: moved_row(copies, sy, x, shift_z, parity),
        lambda sy, x, j: below[sy, x - 2, j],
        (rate_ref[0], rate_ref[1]),
        None,
        None,
        lambda x, parity: (own_ref[x, parity], one),
        (*scratch, weighted, totals),
    )


def join_kernel(low_ref, high_ref, rim_ref, left_ref, right_ref, rim_out, left_out, right_out):
    lane = lanes()
    place = (lane % 32) // 4
    for x in range(12):
        for parity in range(2):
            value = rim_ref[x, parity]
            if x < HALO:
                value = value + to_strips(low_ref[x, parity], 0)
            if x >= 8:
                value = value + to_strips(high_ref[x - 8, parity], 3)
            rim_out[x, parity] = value
    for ref, out, column in ((left_ref, left_out, 0), (right_ref, right_out, 124)):
        out[1] = ref[1]
        for group, halo, chunk in ((0, low_ref, 0), (2, high_ref, 3)):
            message = ref[group]
            for slot in range(8):
                here = (place == slot) & (lane // 32 == chunk)
                message = jnp.where(here, lane_roll(halo[slot // 2, slot % 2], 32 * chunk + 4 * slot - column), message)
            out[group] = message


def outer_kernel(edge_ref, own_ref, low_ref, high_ref, copies, rate_ref, inner_w, inner_t, mid_ref, far, below, squares, halo, *scratch):
    def row(x, parity):
        if x < 0:
            return low_ref[x + HALO, parity]
        return own_ref[x, parity] if x < 16 else high_ref[x - 16, parity]

    def moved(sy, x, shift_z, parity):
        if 0 <= x < 16:
            return moved_row(copies, sy, x, shift_z, parity)
        return moved_row(far, sy, x + HALO if x < 0 else x - 12, shift_z, parity)

    def taken(sy, x, j):
        return below[sy, x + 2 if x < 6 else x - 2, j]

    fill_copies(far, 8, lambda x, parity: row(x - HALO if x < HALO else x + 12, parity))
    put_squares(squares, 0, low_ref, 4)
    put_squares(squares, 4, own_ref, 16)
    put_squares(squares, 20, high_ref, 4)
    fill_below(below, squares, ((0, 0, 8), (12, 8, 8)))
    one = jnp.ones((8, 128), F)
    accumulate(
        16,
        outer_segments,
        row,
        moved,
        taken,
        (rate_ref[0], rate_ref[1]),
        (one * edge_ref[0], one * edge_ref[1]),
        None,
        lambda x, parity: (inner_w[x, parity], inner_t[x, parity]),
        scratch,
    )
    for x in range(16):
        for parity in range(2):
            mid_ref[x, parity] = scratch[-2][x, parity] / scratch[-1][x, parity]


def rim_kernel(edge_ref, rim_ref, left_ref, right_ref, rate_ref, mid_ref, out_ref, rows, copies, below, squares, column_mask, *scratch):
    lane = lanes()
    spot = lane % 32
    for x in range(12):
        group, slot = x // 4, (x % 4) * 2
        for parity in range(2):
            value = rim_ref[x, parity]
            value = jnp.where(spot < 4, lane_roll(left_ref[group], -4 * (slot + parity)), value)
            rows[x, parity] = jnp.where((spot >= 24) & (spot < 28), lane_roll(right_ref[group], 24 - 4 * (slot + parity)), value)
    for sy in range(5):
        off_left = (spot < 4) | ((spot + sy - 2 < 4) & (spot < 16))
        c = spot - 16
        off_right = (c >= 8) | ((c + sy - 2 >= 8) & (c >= 0))
        column_mask[sy] = jnp.where(off_left, edge_ref[2], 1.0) * jnp.where(off_right, edge_ref[3], 1.0)

    def row(x, parity):
        return rows[x + HALO, parity]

    fill_copies(copies, 12, lambda x, parity: rows[x, parity])
    put_squares(squares, 0, rows, 12)
    fill_below(below, squares, ((0, 0, 8),))
    one = jnp.ones((8, 128), F)
    accumulate(
        4,
        whole_segments(4),
        row,
        lambda sy, x, shift_z, parity: moved_row(copies, sy, x + HALO, shift_z, parity),
        lambda sy, x, j: below[sy, x + 2, j],
        (rate_ref[0], rate_ref[1]),
        (jnp.where(lane < 32, edge_ref[0], 1.0), jnp.where(lane >= 96, edge_ref[1], 1.0)),
        column_mask,
        lambda x, parity: (rows[x + HALO, parity], one),
        scratch,
    )
    flat = out_ref.reshape(256, 128)
    for x in range(4):
        for parity in range(2):
            value = scratch[-2][x, parity] / scratch[-1][x, parity]
            for chunk in range(4):
                at = 4 * chunk + x
                edge = jnp.where(lane < 4, lane_roll(value, -32 * chunk - 4), lane_roll(value, 104 - 32 * chunk))
                flat[pl.ds(parity * 16 + at, 8, stride=32)] = jnp.where((lane < 4) | (lane >= 124), edge, mid_ref[at, parity])


def shape(*dims):
    return jax.ShapeDtypeStruct(dims, F)


def call(kernel, name, outs, scratch, mib, in_specs, flops=0):
    return pl.pallas_call(
        kernel,
        out_shape=outs,
        in_specs=[pl.BlockSpec(memory_space=pltpu.SMEM if s else pltpu.VMEM) for s in in_specs],
        out_specs=jax.tree.map(lambda _: pl.BlockSpec(memory_space=pltpu.VMEM), outs),
        scratch_shapes=scratch,
        compiler_params=pltpu.CompilerParams(vmem_limit_bytes=mib * 2**20),
        cost_estimate=pl.CostEstimate(flops=flops, bytes_accessed=500_000, transcendentals=0),
        name=name,
    )


def passed_along(value, axis, steps):
    count = lax.axis_size(axis)
    first, last = max(0, -steps), min(count, count - steps)
    return lax.ppermute(value, axis, [(a, a + steps) for a in range(first, last)])


def per_device(noisy, strength):
    V = pltpu.VMEM
    gx, gy = lax.axis_index("gx"), lax.axis_index("gy")
    edges = jnp.stack([gx > 0, gx < lax.axis_size("gx") - 1, gy > 0, gy < lax.axis_size("gy") - 1]).astype(F)
    row4, row12, row16, three = shape(4, 2, 8, 128), shape(12, 2, 8, 128), shape(16, 2, 8, 128), shape(3, 8, 128)
    copied = (5, 16, 2, 16, 128)
    own, first, last, rate = call(pack_kernel, "pack", (row16, row4, row4, shape(2, 8, 128)), [], 4, (1, 0))(strength, noisy)
    low = passed_along(last, "gx", 1)
    high = passed_along(first, "gx", -1)
    copies, inner_w, inner_t, rim, to_left, to_right = call(
        inner_kernel,
        "inner",
        (shape(*copied), row16, row16, row12, three, three),
        [V((5, 12, 3, 8, 128), F), V((2, 24, 128), F)] + work(16, 16),
        20,
        (0, 0),
        60_000_000,
    )(own, rate)
    rim, to_left, to_right = call(join_kernel, "join", (row12, three, three), [], 4, (0,) * 5)(low, high, rim, to_left, to_right)
    left = passed_along(to_right, "gy", 1)
    right = passed_along(to_left, "gy", -1)
    mid = call(
        outer_kernel,
        "outer",
        row16,
        [V((5, 8, 2, 16, 128), F), V((5, 16, 3, 8, 128), F), V((2, 32, 128), F), V((8, 128), F)]
        + work(16, 8)
        + [V((16, 2, 8, 128), F)] * 2,
        20,
        (1,) + (0,) * 7,
        40_000_000,
    )(edges, own, low, high, copies, rate, inner_w, inner_t)
    return call(
        rim_kernel,
        "rim",
        shape(16, 16, 128),
        [V((12, 2, 8, 128), F), V((5, 12, 2, 16, 128), F), V((5, 8, 3, 8, 128), F), V((2, 24, 128), F), V((5, 8, 128), F)]
        + work(4, 8)
        + [V((4, 2, 8, 128), F)] * 2,
        20,
        (1,) + (0,) * 5,
        20_000_000,
    )(edges, rim, left, right, rate, mid)


def solution(mesh):
    placed = (P(None, "gx", "gy"), P())
    return jax.shard_map(per_device, mesh=mesh, in_specs=placed, out_specs=P(None, "gx", "gy"), check_vma=False)
```

profile of v0, /device:TPU:25, one launch (start us, length us, event | category | flops | bytes accessed | tf_op | source)
XLA Modules:
  0.0 34.6 jit_solution(8676795481501759634)
XLA Ops:
  0.0 0.0 copy-start
  0.0 0.9 %copy-done = f32[16,16,128]{2,1,0:T(8,128)S(1)} copy-done((f32[16,16,128]{2,1,0:T(8,128)S(1)}, f32[16,16,128]{2,1,0:T(8,128)}, u32[]{:S(2)}) %copy-start) | copy-done | bytes 131096
  0.9 0.0 copy-start.1
  0.9 0.7 %copy-done.1 = f32[16]{0:T(128)S(1)} copy-done((f32[16]{0:T(128)S(1)}, f32[16]{0:T(128)}, u32[]{:S(2)}) %copy-start.1) | copy-done | bytes 88
  1.6 0.6 %pack.1 = (f32[16,2,8,128]{3,2,1,0:T(8,128)S(1)}, f32[4,2,8,128]{3,2,1,0:T(8,128)S(1)}, f32[4,2,8,128]{3,2,1,0:T(8,128)S(1)}, f32[2,8,128]{2,1,0:T(8,128)S(1)}) custom-call(f32[16]{0:T(128)S(1)} %copy-done.1, f32[16,16,128]{2,1,0:T(8,128)S(1)} %copy-done), custom_call_target="tpu_custom_call" | custom-call | bytes 500000 | tf_op jit(solution)/shard_map/pack/pallas_call | solution.py:433
  2.2 3.1 %collective-permute-start = (f32[4,2,8,128]{3,2,1,0:T(8,128)S(1)}, f32[4,2,8,128]{3,2,1,0:T(8,128)S(1)}, u32[]{:S(2)}, u32[]{:S(2)}) collective-permute-start(f32[4,2,8,128]{3,2,1,0:T(8,128)S(1)} %get-tuple-element.18), channel_id=1, source_target_pairs={{0,4},{4,8},{8,12},{12,16},{16,20},{20,24},{24,28},{28,32},{32,36}... | collective-permute-start | bytes 98312 | tf_op jit(solution)/shard_map/ppermute | solution.py:424
  5.3 5.2 %collective-permute-start.1 = (f32[4,2,8,128]{3,2,1,0:T(8,128)S(1)}, f32[4,2,8,128]{3,2,1,0:T(8,128)S(1)}, u32[]{:S(2)}, u32[]{:S(2)}) collective-permute-start(f32[4,2,8,128]{3,2,1,0:T(8,128)S(1)} %get-tuple-element.19), channel_id=1, source_target_pairs={{4,0},{8,4},{12,8},{16,12},{20,16},{24,20},{28,24},{32,28},{36,32}... | collective-permute-start | bytes 98312 | tf_op jit(solution)/shard_map/ppermute | solution.py:424
  10.5 6.4 %inner.1 = (f32[5,16,2,16,128]{4,3,2,1,0:T(8,128)S(1)}, f32[16,2,8,128]{3,2,1,0:T(8,128)S(1)}, f32[16,2,8,128]{3,2,1,0:T(8,128)S(1)}, f32[12,2,8,128]{3,2,1,0:T(...) custom-call(f32[16,2,8,128]{3,2,1,0:T(8,128)S(1)} %get-tuple-element.20.own_ref, ...), custom_call_target="tpu_custom_call" | custom-call | flops 60000000 | bytes 500000 | tf_op jit(solution)/shard_map/inner/pallas_call | solution.py:436
  16.9 0.0 collective-permute-done.low_ref
  16.9 0.0 collective-permute-done.1.high_ref
  16.9 0.1 join.1
  17.1 6.6 %collective-permute-start.2 = (f32[3,8,128]{2,1,0:T(8,128)S(1)}, f32[3,8,128]{2,1,0:T(8,128)S(1)}, u32[]{:S(2)}, u32[]{:S(2)}) collective-permute-start(f32[3,8,128]{2,1,0:T(8,128)S(1)} %get-tuple-element.26), channel_id=1, source_target_pairs={{0,1},{1,2},{2,3},{4,5},{5,6},{6,7},{8,9},{9,10},{10,11},{12,13},{... | collective-permute-start | bytes 36872 | tf_op jit(solution)/shard_map/ppermute | solution.py:424
  23.7 2.1 %collective-permute-start.3 = (f32[3,8,128]{2,1,0:T(8,128)S(1)}, f32[3,8,128]{2,1,0:T(8,128)S(1)}, u32[]{:S(2)}, u32[]{:S(2)}) collective-permute-start(f32[3,8,128]{2,1,0:T(8,128)S(1)} %get-tuple-element.27), channel_id=1, source_target_pairs={{1,0},{2,1},{3,2},{5,4},{6,5},{7,6},{9,8},{10,9},{11,10},{13,12},{... | collective-permute-start | bytes 36872 | tf_op jit(solution)/shard_map/ppermute | solution.py:424
  25.8 0.1 add_convert_fusion.edge_ref
  25.9 4.2 %outer.1.mid_ref = f32[16,2,8,128]{3,2,1,0:T(8,128)S(1)} custom-call(f32[4]{0:T(128)S(1)} %add_convert_fusion.edge_ref, f32[16,2,8,128]{3,2,1,0:T(8,128)S(1)} %get-tuple-element.20.own_ref, f32[4,2,8,128]{3,2,1,0:T(8,128)S(1)} %collective-permute-done.low_ref, f32[4,2,8,128]{3,2,1,0:T(8,128)S(1)} %collective-permute-done.1.high_ref, ...), custom_call_target="tpu_custom_call" | custom-call | flops 40000000 | bytes 500000 | tf_op jit(solution)/shard_map/outer/pallas_call | solution.py:448
  30.2 0.0 collective-permute-done.2.left_ref
  30.2 0.1 collective-permute-done.3.right_ref
  30.2 4.4 %rim.1 = f32[16,16,128]{2,1,0:T(8,128)} custom-call(f32[4]{0:T(128)S(1)} %add_convert_fusion.edge_ref, f32[12,2,8,128]{3,2,1,0:T(8,128)S(1)} %get-tuple-element.25.rim_ref, f32[3,8,128]{2,1,0:T(8,128)S(1)} %collective-permute-done.2.left_ref, f32[3,8,128]{2,1,0:T(8,128)S(1)} %collective-permute-done.3.right_ref, ...), custom_call_target="tpu_custom_call" | custom-call | flops 20000000 | bytes 500000 | tf_op jit(solution)/shard_map/rim/pallas_call | solution.py:459
Async XLA Ops:
  0.0 0.9 %copy-start = (f32[16,16,128]{2,1,0:T(8,128)S(1)}, f32[16,16,128]{2,1,0:T(8,128)}, u32[]{:S(2)}) copy-start(f32[16,16,128]{2,1,0:T(8,128)} %noisy_ref.1) | copy-start | bytes 393220
  0.9 0.7 %copy-start.1 = (f32[16]{0:T(128)S(1)}, f32[16]{0:T(128)}, u32[]{:S(2)}) copy-start(f32[16]{0:T(128)} %strength_ref.1) | copy-start | bytes 196
  2.2 14.7 %collective-permute-start = (f32[4,2,8,128]{3,2,1,0:T(8,128)S(1)}, f32[4,2,8,128]{3,2,1,0:T(8,128)S(1)}, u32[]{:S(2)}, u32[]{:S(2)}) collective-permute-start(f32[4,2,8,128]{3,2,1,0:T(8,128)S(1)} %get-tuple-element.18), channel_id=1, source_target_pairs={{0,4},{4,8},{8,12},{12,16},{16,20},{20,24},{24,28},{28,32},{32,36}... | collective-permute-start | bytes 98312 | tf_op jit(solution)/shard_map/ppermute | solution.py:424
  5.3 11.6 %collective-permute-start.1 = (f32[4,2,8,128]{3,2,1,0:T(8,128)S(1)}, f32[4,2,8,128]{3,2,1,0:T(8,128)S(1)}, u32[]{:S(2)}, u32[]{:S(2)}) collective-permute-start(f32[4,2,8,128]{3,2,1,0:T(8,128)S(1)} %get-tuple-element.19), channel_id=1, source_target_pairs={{4,0},{8,4},{12,8},{16,12},{20,16},{24,20},{28,24},{32,28},{36,32}... | collective-permute-start | bytes 98312 | tf_op jit(solution)/shard_map/ppermute | solution.py:424
  17.1 13.1 %collective-permute-start.2 = (f32[3,8,128]{2,1,0:T(8,128)S(1)}, f32[3,8,128]{2,1,0:T(8,128)S(1)}, u32[]{:S(2)}, u32[]{:S(2)}) collective-permute-start(f32[3,8,128]{2,1,0:T(8,128)S(1)} %get-tuple-element.26), channel_id=1, source_target_pairs={{0,1},{1,2},{2,3},{4,5},{5,6},{6,7},{8,9},{9,10},{10,11},{12,13},{... | collective-permute-start | bytes 36872 | tf_op jit(solution)/shard_map/ppermute | solution.py:424
  23.7 6.5 %collective-permute-start.3 = (f32[3,8,128]{2,1,0:T(8,128)S(1)}, f32[3,8,128]{2,1,0:T(8,128)S(1)}, u32[]{:S(2)}, u32[]{:S(2)}) collective-permute-start(f32[3,8,128]{2,1,0:T(8,128)S(1)} %get-tuple-element.27), channel_id=1, source_target_pairs={{1,0},{2,1},{3,2},{5,4},{6,5},{7,6},{9,8},{10,9},{11,10},{13,12},{... | collective-permute-start | bytes 36872 | tf_op jit(solution)/shard_map/ppermute | solution.py:424
where the time goes:
time: 34.8 us; the launch traced here: 34.6 us
  starting transfers between devices  17 us (49%)
  Pallas kernels  15.8 us (45%)
  local copies, waits for them, and re-layouts  1.56 us (4%)
    ppermute x4, starting transfers between devices, passed_along(): lax.ppermute(value, axis, [(a, a + steps) for a in range(first, last)])  17 us
    pallas_call x1, Pallas kernels, per_device(): call(inner_kernel, 'inner', (shape(*copied), row16, row16, row12, three,...  6.4 us
    pallas_call x1, Pallas kernels, per_device(): call(rim_kernel, 'rim', shape(16, 16, 128), [V((12, 2, 8, 128), F), V((5,...  4.37 us
    pallas_call x1, Pallas kernels, per_device(): call(outer_kernel, 'outer', row16, [V((5, 8, 2, 16, 128), F), V((5, 16, 3...  4.25 us
    unnamed x4, local copies, waits for them, and re-layouts  1.56 us
  transfers between devices with their start and end apart: 4, of which 1 were waited for; matrix products, arithmetic and copies ran while one was open for 0% of the time, Pallas kernels for 31%

commit v1 on v0

--- a/solution.py
+++ b/solution.py
@@ -220,24 +220,6 @@
     ]
 
 
-def pack_kernel(strength_ref, noisy_ref, own_ref, first_ref, last_ref, rate_ref):
-    flat = noisy_ref.reshape(256, 128)
-    for x in range(16):
-        for parity in range(2):
-            value = flat[pl.ds(parity * 16 + x, 8, stride=32)]
-            own_ref[x, parity] = value
-            if x < HALO:
-                first_ref[x, parity] = value
-            if x >= 16 - HALO:
-                last_ref[x - 16 + HALO, parity] = value
-    sublane = lax.broadcasted_iota(jnp.int32, (8, 128), 0)
-    for parity in range(2):
-        strength = jnp.full((8, 128), 1.0, F)
-        for s in range(8):
-            strength = jnp.where(sublane == s, strength_ref[2 * s + parity], strength)
-        rate_ref[parity] = (-math.log2(math.e) / 125.0) / strength
-
-
 def inner_segments(shift_x):
     return ((2 + max(0, -shift_x), 12 - abs(shift_x)),)
 
@@ -257,9 +239,19 @@
     return jnp.where((lane >= 4) & (lane < 12), lane_roll(value, 4 + 32 * chunk), right)
 
 
-def inner_kernel(own_ref, rate_ref, copies, weighted, totals, rim_ref, left_ref, right_ref, below, squares, *scratch):
+def inner_kernel(noisy_ref, strength_ref, own_ref, rate_ref, copies, weighted, totals, rim_ref, left_ref, right_ref, below, squares, *scratch):
     def row(x, parity):
         return own_ref[x, parity]
+
+    flat = noisy_ref.reshape(256, 128)
+    for x in range(16):
+        for parity in range(2):
+            own_ref[x, parity] = flat[pl.ds(parity * 16 + x, 8, stride=32)]
+    slices = jnp.broadcast_to(strength_ref[...], (8, 16))
+    sublane, lane = [lax.broadcasted_iota(jnp.int32, (8, 16), dim) for dim in range(2)]
+    for parity in range(2):
+        strength = jnp.sum(jnp.where(lane == 2 * sublane + parity, slices, 0.0), axis=1, keepdims=True)
+        rate_ref[parity] = jnp.broadcast_to((-math.log2(math.e) / 125.0) / strength, (8, 128))
 
     fill_copies(copies, 16, row)
     put_squares(squares, 0, own_ref, 16)
@@ -299,7 +291,15 @@
     )
 
 
-def join_kernel(low_ref, high_ref, rim_ref, left_ref, right_ref, rim_out, left_out, right_out):
+def join_kernel(flag_ref, pair_ref, next_ref, rim_ref, left_ref, right_ref, low_ref, high_ref, rim_out, first_out, second_out):
+    odd = flag_ref[4] > 0.5
+    pair, other = pair_ref.reshape(256, 128), next_ref.reshape(256, 128)
+    for x in range(HALO):
+        for parity in range(2):
+            line = pl.ds(parity * 16 + 12 + x, 8, stride=32)
+            low_ref[x, parity] = jnp.where(odd, pair[line], other[line])
+            line = pl.ds(parity * 16 + x, 8, stride=32)
+            high_ref[x, parity] = jnp.where(odd, other[line], pair[line])
     lane = lanes()
     place = (lane % 32) // 4
     for x in range(12):
@@ -310,17 +310,23 @@
             if x >= 8:
                 value = value + to_strips(high_ref[x - 8, parity], 3)
             rim_out[x, parity] = value
-    for ref, out, column in ((left_ref, left_out, 0), (right_ref, right_out, 124)):
-        out[1] = ref[1]
+    messages = []
+    for ref, column in ((left_ref, 0), (right_ref, 124)):
+        groups = [ref[0], ref[1], ref[2]]
         for group, halo, chunk in ((0, low_ref, 0), (2, high_ref, 3)):
-            message = ref[group]
             for slot in range(8):
                 here = (place == slot) & (lane // 32 == chunk)
-                message = jnp.where(here, lane_roll(halo[slot // 2, slot % 2], 32 * chunk + 4 * slot - column), message)
-            out[group] = message
-
-
-def outer_kernel(edge_ref, own_ref, low_ref, high_ref, copies, rate_ref, inner_w, inner_t, mid_ref, far, below, squares, halo, *scratch):
+                piece = lane_roll(halo[slot // 2, slot % 2], 32 * chunk + 4 * slot - column)
+                groups[group] = jnp.where(here, piece, groups[group])
+        messages.append(groups)
+    odd = flag_ref[5] > 0.5
+    for group in range(3):
+        left, right = messages[0][group], messages[1][group]
+        first_out[group] = jnp.where(odd, left, right)
+        second_out[group] = jnp.where(odd, right, left)
+
+
+def outer_kernel(flag_ref, own_ref, low_ref, high_ref, copies, rate_ref, inner_w, inner_t, mid_ref, far, below, squares, halo, *scratch):
     def row(x, parity):
         if x < 0:
             return low_ref[x + HALO, parity]
@@ -347,7 +353,7 @@
         moved,
         taken,
         (rate_ref[0], rate_ref[1]),
-        (one * edge_ref[0], one * edge_ref[1]),
+        (flag_ref[0], flag_ref[1]),
         None,
         lambda x, parity: (inner_w[x, parity], inner_t[x, parity]),
         scratch,
@@ -357,20 +363,24 @@
             mid_ref[x, parity] = scratch[-2][x, parity] / scratch[-1][x, parity]
 
 
-def rim_kernel(edge_ref, rim_ref, left_ref, right_ref, rate_ref, mid_ref, out_ref, rows, copies, below, squares, column_mask, *scratch):
+def rim_kernel(flag_ref, rim_ref, first_ref, second_ref, rate_ref, mid_ref, out_ref, rows, copies, below, squares, column_mask, *scratch):
     lane = lanes()
     spot = lane % 32
+    odd = flag_ref[5] > 0.5
+    sides = [(first_ref[group], second_ref[group]) for group in range(3)]
+    lefts = [jnp.where(odd, a, b) for a, b in sides]
+    rights = [jnp.where(odd, b, a) for a, b in sides]
     for x in range(12):
         group, slot = x // 4, (x % 4) * 2
         for parity in range(2):
             value = rim_ref[x, parity]
-            value = jnp.where(spot < 4, lane_roll(left_ref[group], -4 * (slot + parity)), value)
-            rows[x, parity] = jnp.where((spot >= 24) & (spot < 28), lane_roll(right_ref[group], 24 - 4 * (slot + parity)), value)
+            value = jnp.where(spot < 4, lane_roll(lefts[group], -4 * (slot + parity)), value)
+            rows[x, parity] = jnp.where((spot >= 24) & (spot < 28), lane_roll(rights[group], 24 - 4 * (slot + parity)), value)
     for sy in range(5):
         off_left = (spot < 4) | ((spot + sy - 2 < 4) & (spot < 16))
         c = spot - 16
         off_right = (c >= 8) | ((c + sy - 2 >= 8) & (c >= 0))
-        column_mask[sy] = jnp.where(off_left, edge_ref[2], 1.0) * jnp.where(off_right, edge_ref[3], 1.0)
+        column_mask[sy] = jnp.where(off_left, flag_ref[2], 1.0) * jnp.where(off_right, flag_ref[3], 1.0)
 
     def row(x, parity):
         return rows[x + HALO, parity]
@@ -386,7 +396,7 @@
         lambda sy, x, shift_z, parity: moved_row(copies, sy, x + HALO, shift_z, parity),
         lambda sy, x, j: below[sy, x + 2, j],
         (rate_ref[0], rate_ref[1]),
-        (jnp.where(lane < 32, edge_ref[0], 1.0), jnp.where(lane >= 96, edge_ref[1], 1.0)),
+        (jnp.where(lane < 32, flag_ref[0], 1.0), jnp.where(lane >= 96, flag_ref[1], 1.0)),
         column_mask,
         lambda x, parity: (rows[x + HALO, parity], one),
         scratch,
@@ -405,12 +415,13 @@
     return jax.ShapeDtypeStruct(dims, F)
 
 
-def call(kernel, name, outs, scratch, mib, in_specs, flops=0):
+def call(kernel, name, outs, scratch, mib, flops=0):
+    spec = pl.BlockSpec(memory_space=pltpu.VMEM)
     return pl.pallas_call(
         kernel,
         out_shape=outs,
-        in_specs=[pl.BlockSpec(memory_space=pltpu.SMEM if s else pltpu.VMEM) for s in in_specs],
-        out_specs=jax.tree.map(lambda _: pl.BlockSpec(memory_space=pltpu.VMEM), outs),
+        out_specs=jax.tree.map(lambda _: spec, outs),
+        in_specs=INPUTS[name] * [spec],
         scratch_shapes=scratch,
         compiler_params=pltpu.CompilerParams(vmem_limit_bytes=mib * 2**20),
         cost_estimate=pl.CostEstimate(flops=flops, bytes_accessed=500_000, transcendentals=0),
@@ -418,33 +429,35 @@
     )
 
 
-def passed_along(value, axis, steps):
-    count = lax.axis_size(axis)
-    first, last = max(0, -steps), min(count, count - steps)
-    return lax.ppermute(value, axis, [(a, a + steps) for a in range(first, last)])
+INPUTS = {"inner": 2, "join": 6, "outer": 8, "rim": 6}
+
+
+def swapped(value, axis, first):
+    pairs = [(a, a + 1) for a in range(first, lax.axis_size(axis) - 1, 2)]
+    return lax.ppermute(value, axis, pairs + [(b, a) for a, b in pairs])
 
 
 def per_device(noisy, strength):
     V = pltpu.VMEM
     gx, gy = lax.axis_index("gx"), lax.axis_index("gy")
-    edges = jnp.stack([gx > 0, gx < lax.axis_size("gx") - 1, gy > 0, gy < lax.axis_size("gy") - 1]).astype(F)
+    flags = [gx > 0, gx < lax.axis_size("gx") - 1, gy > 0, gy < lax.axis_size("gy") - 1, gx % 2 == 1, gy % 2 == 1]
+    flags = jnp.broadcast_to(jnp.stack(flags).astype(F)[:, None, None], (6, 8, 128))
     row4, row12, row16, three = shape(4, 2, 8, 128), shape(12, 2, 8, 128), shape(16, 2, 8, 128), shape(3, 8, 128)
-    copied = (5, 16, 2, 16, 128)
-    own, first, last, rate = call(pack_kernel, "pack", (row16, row4, row4, shape(2, 8, 128)), [], 4, (1, 0))(strength, noisy)
-    low = passed_along(last, "gx", 1)
-    high = passed_along(first, "gx", -1)
-    copies, inner_w, inner_t, rim, to_left, to_right = call(
+    pair = swapped(noisy, "gx", 0)
+    other = swapped(noisy, "gx", 1)
+    own, rate, copies, inner_w, inner_t, rim, to_left, to_right = call(
         inner_kernel,
         "inner",
-        (shape(*copied), row16, row16, row12, three, three),
+        (row16, shape(2, 8, 128), shape(5, 16, 2, 16, 128), row16, row16, row12, three, three),
         [V((5, 12, 3, 8, 128), F), V((2, 24, 128), F)] + work(16, 16),
         20,
-        (0, 0),
         60_000_000,
-    )(own, rate)
-    rim, to_left, to_right = call(join_kernel, "join", (row12, three, three), [], 4, (0,) * 5)(low, high, rim, to_left, to_right)
-    left = passed_along(to_right, "gy", 1)
-    right = passed_along(to_left, "gy", -1)
+    )(noisy, strength.reshape(1, 16))
+    low, high, rim, first, second = call(join_kernel, "join", (row4, row4, row12, three, three), [], 4)(
+        flags, pair, other, rim, to_left, to_right
+    )
+    first = swapped(first, "gy", 0)
+    second = swapped(second, "gy", 1)
     mid = call(
         outer_kernel,
         "outer",
@@ -453,9 +466,8 @@
         + work(16, 8)
         + [V((16, 2, 8, 128), F)] * 2,
         20,
-        (1,) + (0,) * 7,
         40_000_000,
-    )(edges, own, low, high, copies, rate, inner_w, inner_t)
+    )(flags, own, low, high, copies, rate, inner_w, inner_t)
     return call(
         rim_kernel,
         "rim",
@@ -464,9 +476,8 @@
         + work(4, 8)
         + [V((4, 2, 8, 128), F)] * 2,
         20,
-        (1,) + (0,) * 5,
         20_000_000,
-    )(edges, rim, left, right, rate, mid)
+    )(flags, rim, first, second, rate, mid)
 
 
 def solution(mesh):

time: 34.8 us -> 29.4 us (0.84)
  starting transfers between devices: 17 us -> 13.1 us
  Pallas kernels: 15.8 us -> 14.3 us
    ppermute x4, starting transfers between devices: 17 us -> 13.1 us  [swapped(): return lax.ppermute(value, axis, pairs + [(b, a) for a, b in pairs])]
    pallas_call x1, Pallas kernels: 4.37 us -> 3.81 us  [per_device(): call(rim_kernel, 'rim', shape(16, 16, 128), [V((12, 2, 8, 128), F), V((5,...]
    pallas_call x1, Pallas kernels: 4.25 us -> 3.75 us  [per_device(): call(outer_kernel, 'outer', row16, [V((5, 8, 2, 16, 128), F), V((5, 16, 3...]
    pallas_call x3 -> x2, Pallas kernels: 7.15 us -> 6.74 us  [the longest x1 6.56 us: per_device(): call(inner_kernel, 'inner', (row16, shape(2, 8, 128), shape(5, 16, 2, 16,...]
  transfers between devices with their start and end apart: 4 -> 4, of which waited for: 1 -> 0; matrix products, arithmetic and copies ran while one was open for 0% -> 0% of each run, Pallas kernels for 31% -> 35%
where the time goes in v1:
time: 29.4 us; the launch traced here: 29.2 us
  Pallas kernels  14.3 us (49%)
  starting transfers between devices  13.1 us (45%)
  local copies, waits for them, and re-layouts  1.74 us (6%)
    ppermute x4, starting transfers between devices, swapped(): return lax.ppermute(value, axis, pairs + [(b, a) for a, b in pairs])  13.1 us
    pallas_call x1, Pallas kernels, per_device(): call(inner_kernel, 'inner', (row16, shape(2, 8, 128), shape(5, 16, 2, 16,...  6.56 us
    pallas_call x1, Pallas kernels, per_device(): call(rim_kernel, 'rim', shape(16, 16, 128), [V((12, 2, 8, 128), F), V((5,...  3.81 us
    pallas_call x1, Pallas kernels, per_device(): call(outer_kernel, 'outer', row16, [V((5, 8, 2, 16, 128), F), V((5, 16, 3...  3.75 us
    unnamed x4, local copies, waits for them, and re-layouts  1.56 us
  transfers between devices with their start and end apart: 4, of which 0 were waited for; matrix products, arithmetic and copies ran while one was open for 0% of the time, Pallas kernels for 35%

profile of v1, /device:TPU:25, one launch (start us, length us, event | category | flops | bytes accessed | tf_op | source)
XLA Modules:
  0.0 29.2 jit_solution(1633074565781604320)
XLA Ops:
  0.0 1.2 %collective-permute-start = (f32[16,16,128]{2,1,0:T(8,128)}, f32[16,16,128]{2,1,0:T(8,128)S(1)}, u32[]{:S(2)}, u32[]{:S(2)}) collective-permute-start(f32[16,16,128]{2,1,0:T(8,128)} %noisy_ref.1), channel_id=1, source_target_pairs={{0,4},{8,12},{16,20},{24,28},{32,36},{40,44},{48,52},{56,60},{64,6... | collective-permute-start | bytes 393224 | tf_op jit(solution)/shard_map/ppermute | solution.py:437
  1.2 5.2 %collective-permute-start.1 = (f32[16,16,128]{2,1,0:T(8,128)}, f32[16,16,128]{2,1,0:T(8,128)S(1)}, u32[]{:S(2)}, u32[]{:S(2)}) collective-permute-start(f32[16,16,128]{2,1,0:T(8,128)} %noisy_ref.1), channel_id=1, source_target_pairs={{4,8},{12,16},{20,24},{28,32},{36,40},{44,48},{52,56},{60,64},{68,... | collective-permute-start | bytes 393224 | tf_op jit(solution)/shard_map/ppermute | solution.py:437
  6.5 0.1 stack.27
  6.6 0.0 copy-start
  6.6 0.9 %copy-done = f32[16,16,128]{2,1,0:T(8,128)S(1)} copy-done((f32[16,16,128]{2,1,0:T(8,128)S(1)}, f32[16,16,128]{2,1,0:T(8,128)}, u32[]{:S(2)}) %copy-start) | copy-done | bytes 131096
  7.5 0.0 copy-start.1
  7.5 0.7 %copy-done.1 = f32[16]{0:T(128)S(1)} copy-done((f32[16]{0:T(128)S(1)}, f32[16]{0:T(128)}, u32[]{:S(2)}) %copy-start.1) | copy-done | bytes 88
  8.2 6.6 %inner.1 = (f32[16,2,8,128]{3,2,1,0:T(8,128)S(1)}, f32[2,8,128]{2,1,0:T(8,128)S(1)}, f32[5,16,2,16,128]{4,3,2,1,0:T(8,128)S(1)}, f32[16,2,8,128]{3,2,1,0:T(8,128...) custom-call(f32[16,16,128]{2,1,0:T(8,128)S(1)} %copy-done, ...), custom_call_target="tpu_custom_call" | custom-call | flops 60000000 | bytes 500000 | tf_op jit(solution)/shard_map/inner/pallas_call | solution.py:448
  14.7 0.0 collective-permute-done.pair_ref
  14.8 0.0 collective-permute-done.1.next_ref
  14.8 0.1 broadcast_in_dim.2.flag_ref
  14.8 0.2 join.1
  15.0 1.3 %collective-permute-start.2 = (f32[3,8,128]{2,1,0:T(8,128)S(1)}, f32[3,8,128]{2,1,0:T(8,128)S(1)}, u32[]{:S(2)}, u32[]{:S(2)}) collective-permute-start(f32[3,8,128]{2,1,0:T(8,128)S(1)} %get-tuple-element.22), channel_id=1, source_target_pairs={{0,1},{2,3},{1,0},{3,2},{4,5},{6,7},{5,4},{7,6},{8,9},{10,11},{9,8... | collective-permute-start | bytes 36872 | tf_op jit(solution)/shard_map/ppermute | solution.py:437
  16.3 5.3 %collective-permute-start.3 = (f32[3,8,128]{2,1,0:T(8,128)S(1)}, f32[3,8,128]{2,1,0:T(8,128)S(1)}, u32[]{:S(2)}, u32[]{:S(2)}) collective-permute-start(f32[3,8,128]{2,1,0:T(8,128)S(1)} %get-tuple-element.23), channel_id=1, source_target_pairs={{1,2},{2,1},{5,6},{6,5},{9,10},{10,9},{13,14},{14,13},{17,18},{18,... | collective-permute-start | bytes 36872 | tf_op jit(solution)/shard_map/ppermute | solution.py:437
  21.6 3.8 %outer.1.mid_ref = f32[16,2,8,128]{3,2,1,0:T(8,128)S(1)} custom-call(f32[6,8,128]{2,1,0:T(8,128)S(1)} %broadcast_in_dim.2.flag_ref, f32[16,2,8,128]{3,2,1,0:T(8,128)S(1)} %get-tuple-element.25.own_ref, f32[4,2,8,128]{3,2,1,0:T(8,128)S(1)} %get-tuple-element.26.low_ref, f32[4,2,8,128]{3,2,1,0:T(8,128)S(1)} %get-tuple-element.27.high_ref, ...), custom_call_target="tpu_custom_call" | custom-call | flops 40000000 | bytes 500000 | tf_op jit(solution)/shard_map/outer/pallas_call | solution.py:461
  25.4 0.0 collective-permute-done.2.first_ref
  25.4 0.0 collective-permute-done.3.second_ref
  25.4 3.8 %rim.1 = f32[16,16,128]{2,1,0:T(8,128)} custom-call(f32[6,8,128]{2,1,0:T(8,128)S(1)} %broadcast_in_dim.2.flag_ref, f32[12,2,8,128]{3,2,1,0:T(8,128)S(1)} %get-tuple-element.21.rim_ref, f32[3,8,128]{2,1,0:T(8,128)S(1)} %collective-permute-done.2.first_ref, f32[3,8,128]{2,1,0:T(8,128)S(1)} %collective-permute-done.3.second_ref, ...), custom_call_target="tpu_custom_call" | custom-call | flops 20000000 | bytes 500000 | tf_op jit(solution)/shard_map/rim/pallas_call | solution.py:471
  (1 shorter events, 0.0 us)
Async XLA Ops:
  0.0 14.7 %collective-permute-start = (f32[16,16,128]{2,1,0:T(8,128)}, f32[16,16,128]{2,1,0:T(8,128)S(1)}, u32[]{:S(2)}, u32[]{:S(2)}) collective-permute-start(f32[16,16,128]{2,1,0:T(8,128)} %noisy_ref.1), channel_id=1, source_target_pairs={{0,4},{8,12},{16,20},{24,28},{32,36},{40,44},{48,52},{56,60},{64,6... | collective-permute-start | bytes 393224 | tf_op jit(solution)/shard_map/ppermute | solution.py:437
  1.2 13.5 %collective-permute-start.1 = (f32[16,16,128]{2,1,0:T(8,128)}, f32[16,16,128]{2,1,0:T(8,128)S(1)}, u32[]{:S(2)}, u32[]{:S(2)}) collective-permute-start(f32[16,16,128]{2,1,0:T(8,128)} %noisy_ref.1), channel_id=1, source_target_pairs={{4,8},{12,16},{20,24},{28,32},{36,40},{44,48},{52,56},{60,64},{68,... | collective-permute-start | bytes 393224 | tf_op jit(solution)/shard_map/ppermute | solution.py:437
  6.6 0.9 %copy-start = (f32[16,16,128]{2,1,0:T(8,128)S(1)}, f32[16,16,128]{2,1,0:T(8,128)}, u32[]{:S(2)}) copy-start(f32[16,16,128]{2,1,0:T(8,128)} %noisy_ref.1) | copy-start | bytes 393220
  7.5 0.7 %copy-start.1 = (f32[16]{0:T(128)S(1)}, f32[16]{0:T(128)}, u32[]{:S(2)}) copy-start(f32[16]{0:T(128)} %param.3) | copy-start | bytes 196
  15.0 10.4 %collective-permute-start.2 = (f32[3,8,128]{2,1,0:T(8,128)S(1)}, f32[3,8,128]{2,1,0:T(8,128)S(1)}, u32[]{:S(2)}, u32[]{:S(2)}) collective-permute-start(f32[3,8,128]{2,1,0:T(8,128)S(1)} %get-tuple-element.22), channel_id=1, source_target_pairs={{0,1},{2,3},{1,0},{3,2},{4,5},{6,7},{5,4},{7,6},{8,9},{10,11},{9,8... | collective-permute-start | bytes 36872 | tf_op jit(solution)/shard_map/ppermute | solution.py:437
  16.3 9.1 %collective-permute-start.3 = (f32[3,8,128]{2,1,0:T(8,128)S(1)}, f32[3,8,128]{2,1,0:T(8,128)S(1)}, u32[]{:S(2)}, u32[]{:S(2)}) collective-permute-start(f32[3,8,128]{2,1,0:T(8,128)S(1)} %get-tuple-element.23), channel_id=1, source_target_pairs={{1,2},{2,1},{5,6},{6,5},{9,10},{10,9},{13,14},{14,13},{17,18},{18,... | collective-permute-start | bytes 36872 | tf_op jit(solution)/shard_map/ppermute | solution.py:437

commit v2 on v1

--- a/solution.py
+++ b/solution.py
@@ -28,62 +28,47 @@
 
 
 def moved_row(copies, sy, row, shift_z, parity):
-    k = shift_z + parity
-    return copies[sy, row, k % 2, k // 2 : k // 2 + 8]
-
-
-def fill_copies(copies, count, row):
-    flat = copies.reshape(5 * count * 2 * 16, 128)
-    for slot in range(0, 10 * count, 8):
+    return copies[sy, row, shift_z + parity]
+
+
+def fill_copies(copies, steps, count, row):
+    flat = steps.reshape(2 * count * 16, 128)
+    for slot in range(0, 2 * count, 8):
         flat[pl.ds(16 * slot + 8, 8, stride=16)] = jnp.zeros((8, 128), F)
     for x in range(count):
         for parity in range(2):
             value = row(x, parity)
+            steps[x, parity, 0:8] = value
+            up = steps[x, parity, 1:9]
             for sy in range(5):
-                copies[sy, x, parity, 0:8] = lane_roll(value, 2 - sy)
-
-
-def fill_below(below, squares, blocks):
-    count = below.shape[1]
-    for sy in range(5):
-        for x in range(count):
-            for j in range(3):
-                below[sy, x, j] = jnp.zeros((8, 128), F)
-    flat = below.reshape(5 * count * 3 * 8, 128)
-    for source, target, many in blocks:
+                copies[sy, x, parity] = lane_roll(value, 2 - sy)
+                copies[sy, x, parity + 2] = lane_roll(up, 2 - sy)
+
+
+def fill_below(below, centers, row):
+    squares = {}
+
+    def square(x):
+        if x not in squares:
+            squares[x] = [row(x, parity) * row(x, parity) for parity in range(2)]
+        return squares[x]
+
+    for place, x in enumerate(centers):
         sums = []
         for parity in range(2):
-            total = squares[parity, source : source + many]
-            for step in range(1, 5):
-                total = total + squares[parity, source + step : source + step + many]
-            near = lane_roll(total, 1) + lane_roll(total, 127)
-            far = lane_roll(total, 2) + lane_roll(total, 126)
-            sums.append(total + near + far)
+            near = square(x - 1)[parity] + square(x + 1)[parity]
+            far = square(x - 2)[parity] + square(x + 2)[parity]
+            sums.append(square(x)[parity] + near + far)
         three = (sums[0], sums[0] + sums[1], sums[1])
         for j in range(3):
             for sy in range(5):
-                flat[pl.ds(((sy * count + target) * 3 + j) * 8, many, stride=24)] = lane_roll(three[j], 2 - sy)
-
-
-def put_squares(squares, at, ref, count):
-    flat = ref.reshape(count * 16, 128)
-    for parity in range(2):
-        for start in range(0, count, 8):
-            many = min(8, count - start)
-            value = flat[pl.ds(parity * 8 + 16 * start, many, stride=16)]
-            squares[parity, at + start : at + start + many] = value * value
-
-
-def clear_sides(sides):
-    slots = sides.shape[0] * sides.shape[1] * 3
-    flat = sides.reshape(slots * 24, 128)
-    for slot in range(0, slots, 8):
-        flat[pl.ds(24 * slot + 7, 8, stride=24)] = jnp.zeros((8, 128), F)
-        flat[pl.ds(24 * slot + 16, 8, stride=24)] = jnp.zeros((8, 128), F)
-
-
-def patch_sums(rows, row, moved, sides, parts, base):
+                below[sy, place, j] = lane_roll(three[j], 2 - sy)
+
+
+def patch_sums(rows, row, moved, under, parts):
     first, count = rows
+    sub = lax.broadcasted_iota(jnp.int32, (8, 128), 0)
+    top, bottom = sub == 0, sub == 7
     squared, pairs, fours = {}, {}, {}
 
     def square(m):
@@ -107,22 +92,20 @@
         shared, other = (four(j + 1), square(j)) if j % 2 == 0 else (four(j), square(j + 4))
         even, odd = [a + b for a, b in zip(shared, other)]
         both = even + odd
-        sides[j, 0, 8:16] = both
-        sides[j, 1, 8:16] = even
-        sides[j, 2, 8:16] = odd
-        even = both + sides[j, 0, 7:15] + sides[j, 1, 9:17]
-        odd = both + sides[j, 0, 9:17] + sides[j, 2, 7:15]
+        up = jnp.where(top, under(first + j, 0), pltpu.roll(both, 1, 0))
+        down = jnp.where(bottom, 0.0, pltpu.roll(both, 7, 0))
+        even, odd = (
+            both + up + jnp.where(bottom, 0.0, pltpu.roll(even, 7, 0)),
+            both + down + jnp.where(top, under(first + j, 1), pltpu.roll(odd, 1, 0)),
+        )
         sums = jnp.concatenate([even, odd], 0)
         high = sums.astype(B)
-        at = base + 16 * j
-        parts[at : at + 16, 0:128] = high
-        parts[at : at + 16, 128:256] = (sums - high.astype(F)).astype(B)
+        parts.append(jnp.concatenate([high, (sums - high.astype(F)).astype(B)], 1))
 
 
 def accumulate(nx, segments, row, moved, below, rates, masks, column_mask, start, scratch):
-    sides, parts, kept, carry, weighted, totals = scratch
+    kept, carry, weighted, totals = scratch
     last_slice = lax.broadcasted_iota(jnp.int32, (8, 128), 0) == 7
-    clear_sides(sides)
     carry_flat = carry.reshape(2 * nx * 4 * 16, 128)
     for slot in range(0, 8 * nx, 8):
         carry_flat[pl.ds(16 * slot + 7, 8, stride=16)] = jnp.zeros((8, 128), F)
@@ -135,7 +118,7 @@
     for sy in range(5):
         place = {}
         for shift_z in range(3):
-            base, todo = 0, []
+            base, todo, parts = 0, [], []
             for n, shift_x in enumerate(offsets(shift_z, sy)):
                 slot = 0
                 for rows in segments(shift_x):
@@ -143,21 +126,18 @@
                         rows,
                         row,
                         lambda x, parity: moved(sy, x + shift_x, shift_z, parity),
-                        sides.at[n, slot : slot + rows[1]],
+                        lambda x, parity: below(sy, x + shift_x, (shift_z - 1) * (1 + parity)) if shift_z else 0.0,
                         parts,
-                        base,
                     )
                     todo.append((shift_x, rows, base, n, slot))
                     base += 16 * rows[1]
                     slot += rows[1]
-            sums = jnp.dot(parts[0:base], band, preferred_element_type=F)
+            sums = jnp.dot(jnp.concatenate(parts, 0), band, preferred_element_type=F)
             for shift_x, rows, at, n, slot in todo:
                 for j in range(rows[1]):
                     x = rows[0] + j
                     for parity in range(2):
                         distance = sums[at + 16 * j + 8 * parity : at + 16 * j + 8 * parity + 8]
-                        if shift_z:
-                            distance = distance + below(sy, x + shift_x, (shift_z - 1) * (1 + parity))
                         weight = jnp.exp2(distance * rates[parity])
                         if x < 0 or x + shift_x < 0:
                             weight = weight * masks[0]
@@ -213,8 +193,6 @@
 
 def work(nx, rows):
     return [
-        pltpu.VMEM((5, rows, 3, 24, 128), F),
-        pltpu.VMEM((5 * 16 * rows, 256), B),
         pltpu.VMEM((2, 15, rows, 2, 8, 128), F),
         pltpu.VMEM((2, nx, 4, 16, 128), F),
     ]
@@ -239,7 +217,7 @@
     return jnp.where((lane >= 4) & (lane < 12), lane_roll(value, 4 + 32 * chunk), right)
 
 
-def inner_kernel(noisy_ref, strength_ref, own_ref, rate_ref, copies, weighted, totals, rim_ref, left_ref, right_ref, below, squares, *scratch):
+def inner_kernel(noisy_ref, slices_ref, own_ref, rate_ref, copies, weighted, totals, rim_ref, left_ref, right_ref, steps, below, *scratch):
     def row(x, parity):
         return own_ref[x, parity]
 
@@ -247,15 +225,8 @@
     for x in range(16):
         for parity in range(2):
             own_ref[x, parity] = flat[pl.ds(parity * 16 + x, 8, stride=32)]
-    slices = jnp.broadcast_to(strength_ref[...], (8, 16))
-    sublane, lane = [lax.broadcasted_iota(jnp.int32, (8, 16), dim) for dim in range(2)]
-    for parity in range(2):
-        strength = jnp.sum(jnp.where(lane == 2 * sublane + parity, slices, 0.0), axis=1, keepdims=True)
-        rate_ref[parity] = jnp.broadcast_to((-math.log2(math.e) / 125.0) / strength, (8, 128))
-
-    fill_copies(copies, 16, row)
-    put_squares(squares, 0, own_ref, 16)
-    fill_below(below, squares, ((0, 0, 8), (8, 8, 4)))
+    fill_copies(copies, steps, 16, row)
+    fill_below(below, range(2, 14), row)
     lane = lanes()
     place = (lane % 32) // 4
     for x in range(12):
@@ -276,6 +247,12 @@
                         here = (place == slot) & (lane // 32 == chunk)
                         message = jnp.where(here, lane_roll(own_ref[source, slot % 2], 32 * chunk + 4 * slot - column), message)
             ref[group] = message
+    slices = jnp.broadcast_to(slices_ref[...], (8, 16))
+    sublane, lane = [lax.broadcasted_iota(jnp.int32, (8, 16), dim) for dim in range(2)]
+    for parity in range(2):
+        rate = jnp.sum(jnp.where(lane == 2 * sublane + parity, slices, 0.0), axis=1, keepdims=True)
+        rate_ref[parity] = jnp.broadcast_to(rate, (8, 128))
+
     one = jnp.ones((8, 128), F)
     accumulate(
         16,
@@ -291,8 +268,8 @@
     )
 
 
-def join_kernel(flag_ref, pair_ref, next_ref, rim_ref, left_ref, right_ref, low_ref, high_ref, rim_out, first_out, second_out):
-    odd = flag_ref[4] > 0.5
+def join_kernel(pair_ref, next_ref, rim_ref, left_ref, right_ref, low_ref, high_ref, rim_out, first_out, second_out):
+    odd = flag("odd_x") > 0.5
     pair, other = pair_ref.reshape(256, 128), next_ref.reshape(256, 128)
     for x in range(HALO):
         for parity in range(2):
@@ -319,14 +296,14 @@
                 piece = lane_roll(halo[slot // 2, slot % 2], 32 * chunk + 4 * slot - column)
                 groups[group] = jnp.where(here, piece, groups[group])
         messages.append(groups)
-    odd = flag_ref[5] > 0.5
+    odd = flag("odd_y") > 0.5
     for group in range(3):
         left, right = messages[0][group], messages[1][group]
         first_out[group] = jnp.where(odd, left, right)
         second_out[group] = jnp.where(odd, right, left)
 
 
-def outer_kernel(flag_ref, own_ref, low_ref, high_ref, copies, rate_ref, inner_w, inner_t, mid_ref, far, below, squares, halo, *scratch):
+def outer_kernel(own_ref, low_ref, high_ref, copies, rate_ref, inner_w, inner_t, mid_ref, far, steps, below, *scratch):
     def row(x, parity):
         if x < 0:
             return low_ref[x + HALO, parity]
@@ -340,11 +317,8 @@
     def taken(sy, x, j):
         return below[sy, x + 2 if x < 6 else x - 2, j]
 
-    fill_copies(far, 8, lambda x, parity: row(x - HALO if x < HALO else x + 12, parity))
-    put_squares(squares, 0, low_ref, 4)
-    put_squares(squares, 4, own_ref, 16)
-    put_squares(squares, 20, high_ref, 4)
-    fill_below(below, squares, ((0, 0, 8), (12, 8, 8)))
+    fill_copies(far, steps, 8, lambda x, parity: row(x - HALO if x < HALO else x + 12, parity))
+    fill_below(below, [*range(-2, 6), *range(10, 18)], row)
     one = jnp.ones((8, 128), F)
     accumulate(
         16,
@@ -353,7 +327,7 @@
         moved,
         taken,
         (rate_ref[0], rate_ref[1]),
-        (flag_ref[0], flag_ref[1]),
+        (flag("below"), flag("above")),
         None,
         lambda x, parity: (inner_w[x, parity], inner_t[x, parity]),
         scratch,
@@ -363,10 +337,10 @@
             mid_ref[x, parity] = scratch[-2][x, parity] / scratch[-1][x, parity]
 
 
-def rim_kernel(flag_ref, rim_ref, first_ref, second_ref, rate_ref, mid_ref, out_ref, rows, copies, below, squares, column_mask, *scratch):
+def rim_kernel(rim_ref, first_ref, second_ref, rate_ref, mid_ref, out_ref, rows, copies, steps, below, column_mask, *scratch):
     lane = lanes()
     spot = lane % 32
-    odd = flag_ref[5] > 0.5
+    odd = flag("odd_y") > 0.5
     sides = [(first_ref[group], second_ref[group]) for group in range(3)]
     lefts = [jnp.where(odd, a, b) for a, b in sides]
     rights = [jnp.where(odd, b, a) for a, b in sides]
@@ -380,14 +354,13 @@
         off_left = (spot < 4) | ((spot + sy - 2 < 4) & (spot < 16))
         c = spot - 16
         off_right = (c >= 8) | ((c + sy - 2 >= 8) & (c >= 0))
-        column_mask[sy] = jnp.where(off_left, flag_ref[2], 1.0) * jnp.where(off_right, flag_ref[3], 1.0)
+        column_mask[sy] = jnp.where(off_left, flag("left"), 1.0) * jnp.where(off_right, flag("right"), 1.0)
 
     def row(x, parity):
         return rows[x + HALO, parity]
 
-    fill_copies(copies, 12, lambda x, parity: rows[x, parity])
-    put_squares(squares, 0, rows, 12)
-    fill_below(below, squares, ((0, 0, 8),))
+    fill_copies(copies, steps, 12, lambda x, parity: rows[x, parity])
+    fill_below(below, range(-2, 6), row)
     one = jnp.ones((8, 128), F)
     accumulate(
         4,
@@ -396,7 +369,7 @@
         lambda sy, x, shift_z, parity: moved_row(copies, sy, x + HALO, shift_z, parity),
         lambda sy, x, j: below[sy, x + 2, j],
         (rate_ref[0], rate_ref[1]),
-        (jnp.where(lane < 32, flag_ref[0], 1.0), jnp.where(lane >= 96, flag_ref[1], 1.0)),
+        (jnp.where(lane < 32, flag("below"), 1.0), jnp.where(lane >= 96, flag("above"), 1.0)),
         column_mask,
         lambda x, parity: (rows[x + HALO, parity], one),
         scratch,
@@ -409,6 +382,19 @@
                 at = 4 * chunk + x
                 edge = jnp.where(lane < 4, lane_roll(value, -32 * chunk - 4), lane_roll(value, 104 - 32 * chunk))
                 flat[pl.ds(parity * 16 + at, 8, stride=32)] = jnp.where((lane < 4) | (lane >= 124), edge, mid_ref[at, parity])
+
+
+def flag(what):
+    gx, gy = lax.axis_index("gx"), lax.axis_index("gy")
+    holds = {
+        "below": gx > 0,
+        "above": gx < lax.axis_size("gx") - 1,
+        "left": gy > 0,
+        "right": gy < lax.axis_size("gy") - 1,
+        "odd_x": gx % 2 == 1,
+        "odd_y": gy % 2 == 1,
+    }
+    return jnp.full((8, 128), jnp.where(holds[what], 1.0, 0.0), F)
 
 
 def shape(*dims):
@@ -429,7 +415,7 @@
     )
 
 
-INPUTS = {"inner": 2, "join": 6, "outer": 8, "rim": 6}
+INPUTS = {"inner": 2, "join": 5, "outer": 7, "rim": 5}
 
 
 def swapped(value, axis, first):
@@ -439,22 +425,20 @@
 
 def per_device(noisy, strength):
     V = pltpu.VMEM
-    gx, gy = lax.axis_index("gx"), lax.axis_index("gy")
-    flags = [gx > 0, gx < lax.axis_size("gx") - 1, gy > 0, gy < lax.axis_size("gy") - 1, gx % 2 == 1, gy % 2 == 1]
-    flags = jnp.broadcast_to(jnp.stack(flags).astype(F)[:, None, None], (6, 8, 128))
     row4, row12, row16, three = shape(4, 2, 8, 128), shape(12, 2, 8, 128), shape(16, 2, 8, 128), shape(3, 8, 128)
+    rates = ((-math.log2(math.e) / 125.0) / strength).reshape(1, 16)
     pair = swapped(noisy, "gx", 0)
     other = swapped(noisy, "gx", 1)
     own, rate, copies, inner_w, inner_t, rim, to_left, to_right = call(
         inner_kernel,
         "inner",
-        (row16, shape(2, 8, 128), shape(5, 16, 2, 16, 128), row16, row16, row12, three, three),
-        [V((5, 12, 3, 8, 128), F), V((2, 24, 128), F)] + work(16, 16),
+        (row16, shape(2, 8, 128), shape(5, 16, 5, 8, 128), row16, row16, row12, three, three),
+        [V((16, 2, 16, 128), F), V((5, 12, 3, 8, 128), F)] + work(16, 16),
         20,
         60_000_000,
-    )(noisy, strength.reshape(1, 16))
+    )(noisy, rates)
     low, high, rim, first, second = call(join_kernel, "join", (row4, row4, row12, three, three), [], 4)(
-        flags, pair, other, rim, to_left, to_right
+        pair, other, rim, to_left, to_right
     )
     first = swapped(first, "gy", 0)
     second = swapped(second, "gy", 1)
@@ -462,22 +446,22 @@
         outer_kernel,
         "outer",
         row16,
-        [V((5, 8, 2, 16, 128), F), V((5, 16, 3, 8, 128), F), V((2, 32, 128), F), V((8, 128), F)]
+        [V((5, 8, 5, 8, 128), F), V((8, 2, 16, 128), F), V((5, 16, 3, 8, 128), F)]
         + work(16, 8)
         + [V((16, 2, 8, 128), F)] * 2,
         20,
         40_000_000,
-    )(flags, own, low, high, copies, rate, inner_w, inner_t)
+    )(own, low, high, copies, rate, inner_w, inner_t)
     return call(
         rim_kernel,
         "rim",
         shape(16, 16, 128),
-        [V((12, 2, 8, 128), F), V((5, 12, 2, 16, 128), F), V((5, 8, 3, 8, 128), F), V((2, 24, 128), F), V((5, 8, 128), F)]
+        [V((12, 2, 8, 128), F), V((5, 12, 5, 8, 128), F), V((12, 2, 16, 128), F), V((5, 8, 3, 8, 128), F), V((5, 8, 128), F)]
         + work(4, 8)
         + [V((4, 2, 8, 128), F)] * 2,
         20,
         20_000_000,
-    )(flags, rim, first, second, rate, mid)
+    )(rim, first, second, rate, mid)
 
 
 def solution(mesh):

time: 29.4 us -> 26.1 us (0.89)
  Pallas kernels: 14.3 us -> 11.4 us
  local copies, waits for them, and re-layouts: 1.74 us -> 0.91 us
  other arithmetic: 0.01 us -> 0.66 us
    pallas_call x2, Pallas kernels: 10.3 us -> 8.1 us  [the longest x1 5.06 us: per_device(): call(inner_kernel, 'inner', (row16, shape(2, 8, 128), shape(5, 16, 5, 8,...]
    pallas_call x1, Pallas kernels: 3.81 us -> 3.1 us  [per_device(): call(rim_kernel, 'rim', shape(16, 16, 128), [V((12, 2, 8, 128), F), V((5,...]
    reshape x0 -> x1, other arithmetic: none -> 0.66 us  [per_device(): rates = (-math.log2(math.e) / 125.0 / strength).reshape(1, 16)]
    unnamed x4 -> x2, local copies, waits for them, and re-layouts: 1.56 us -> 0.91 us
  transfers between devices with their start and end apart: 4 -> 4, of which waited for: 0 -> 0; matrix products, arithmetic and copies ran while one was open for 0% -> 3% of each run, Pallas kernels for 35% -> 31%
where the time goes in v2:
time: 26.1 us; the launch traced here: 25.9 us
  starting transfers between devices  12.9 us (49%)
  Pallas kernels  11.4 us (44%)
  local copies, waits for them, and re-layouts  0.91 us (3%)
  other arithmetic  0.66 us (3%)
    ppermute x4, starting transfers between devices, swapped(): return lax.ppermute(value, axis, pairs + [(b, a) for a, b in pairs])  12.9 us
    pallas_call x1, Pallas kernels, per_device(): call(inner_kernel, 'inner', (row16, shape(2, 8, 128), shape(5, 16, 5, 8,...  5.06 us
    pallas_call x1, Pallas kernels, per_device(): call(rim_kernel, 'rim', shape(16, 16, 128), [V((12, 2, 8, 128), F), V((5,...  3.1 us
    pallas_call x1, Pallas kernels, per_device(): call(outer_kernel, 'outer', row16, [V((5, 8, 5, 8, 128), F), V((8, 2, 16,...  3.05 us
    unnamed x2, local copies, waits for them, and re-layouts  0.91 us
    reshape x1, other arithmetic, per_device(): rates = (-math.log2(math.e) / 125.0 / strength).reshape(1, 16)  0.66 us
  transfers between devices with their start and end apart: 4, of which 0 were waited for; matrix products, arithmetic and copies ran while one was open for 3% of the time, Pallas kernels for 31%

profile of v2, /device:TPU:25, one launch (start us, length us, event | category | flops | bytes accessed | tf_op | source)
XLA Modules:
  0.0 25.9 jit_solution(6113105257430905772)
XLA Ops:
  0.0 1.2 %collective-permute-start = (f32[16,16,128]{2,1,0:T(8,128)}, f32[16,16,128]{2,1,0:T(8,128)S(1)}, u32[]{:S(2)}, u32[]{:S(2)}) collective-permute-start(f32[16,16,128]{2,1,0:T(8,128)} %noisy_ref.1), channel_id=1, source_target_pairs={{0,4},{8,12},{16,20},{24,28},{32,36},{40,44},{48,52},{56,60},{64,6... | collective-permute-start | bytes 393224 | tf_op jit(solution)/shard_map/ppermute | solution.py:423
  1.2 5.2 %collective-permute-start.1 = (f32[16,16,128]{2,1,0:T(8,128)}, f32[16,16,128]{2,1,0:T(8,128)S(1)}, u32[]{:S(2)}, u32[]{:S(2)}) collective-permute-start(f32[16,16,128]{2,1,0:T(8,128)} %noisy_ref.1), channel_id=1, source_target_pairs={{4,8},{12,16},{20,24},{28,32},{36,40},{44,48},{52,56},{60,64},{68,... | collective-permute-start | bytes 393224 | tf_op jit(solution)/shard_map/ppermute | solution.py:423
  6.5 0.7 %divide_bitcast_fusion.slices_ref = f32[1,16]{1,0:T(1,128)S(1)} fusion(f32[16]{0:T(128)} %param.3), kind=kLoop, calls=%fused_computation | loop fusion | flops 16 | bytes 128 | tf_op jit(solution)/shard_map/reshape | solution.py:429
  7.1 0.0 copy-start
  7.1 0.9 %copy-done = f32[16,16,128]{2,1,0:T(8,128)S(1)} copy-done((f32[16,16,128]{2,1,0:T(8,128)S(1)}, f32[16,16,128]{2,1,0:T(8,128)}, u32[]{:S(2)}) %copy-start) | copy-done | bytes 131096
  8.0 5.1 %inner.1 = (f32[16,2,8,128]{3,2,1,0:T(8,128)S(1)}, f32[2,8,128]{2,1,0:T(8,128)S(1)}, f32[5,16,5,8,128]{4,3,2,1,0:T(8,128)S(1)}, f32[16,2,8,128]{3,2,1,0:T(8,128)...) custom-call(f32[16,16,128]{2,1,0:T(8,128)S(1)} %copy-done, ...), custom_call_target="tpu_custom_call" | custom-call | flops 60000000 | bytes 500000 | tf_op jit(solution)/shard_map/inner/pallas_call | solution.py:432
  13.1 0.0 collective-permute-done.pair_ref
  13.1 0.0 collective-permute-done.1.next_ref
  13.1 0.2 join.1
  13.3 1.3 %collective-permute-start.2 = (f32[3,8,128]{2,1,0:T(8,128)S(1)}, f32[3,8,128]{2,1,0:T(8,128)S(1)}, u32[]{:S(2)}, u32[]{:S(2)}) collective-permute-start(f32[3,8,128]{2,1,0:T(8,128)S(1)} %get-tuple-element.22), channel_id=1, source_target_pairs={{0,1},{2,3},{1,0},{3,2},{4,5},{6,7},{5,4},{7,6},{8,9},{10,11},{9,8... | collective-permute-start | bytes 36872 | tf_op jit(solution)/shard_map/ppermute | solution.py:423
  14.6 5.1 %collective-permute-start.3 = (f32[3,8,128]{2,1,0:T(8,128)S(1)}, f32[3,8,128]{2,1,0:T(8,128)S(1)}, u32[]{:S(2)}, u32[]{:S(2)}) collective-permute-start(f32[3,8,128]{2,1,0:T(8,128)S(1)} %get-tuple-element.23), channel_id=1, source_target_pairs={{1,2},{2,1},{5,6},{6,5},{9,10},{10,9},{13,14},{14,13},{17,18},{18,... | collective-permute-start | bytes 36872 | tf_op jit(solution)/shard_map/ppermute | solution.py:423
  19.7 3.0 %outer.1.mid_ref = f32[16,2,8,128]{3,2,1,0:T(8,128)S(1)} custom-call(f32[16,2,8,128]{3,2,1,0:T(8,128)S(1)} %get-tuple-element.25.own_ref, f32[4,2,8,128]{3,2,1,0:T(8,128)S(1)} %get-tuple-element.26.low_ref, f32[4,2,8,128]{3,2,1,0:T(8,128)S(1)} %get-tuple-element.27.high_ref, f32[5,16,5,8,128]{4,3,2,1,0:T(8,128)S(1)} %get-tuple-element.28.copies, ...), custom_call_target="tpu_custom_call" | custom-call | flops 40000000 | bytes 500000 | tf_op jit(solution)/shard_map/outer/pallas_call | solution.py:445
  22.8 0.0 collective-permute-done.2.first_ref
  22.8 0.0 collective-permute-done.3.second_ref
  22.8 3.1 %rim.1 = f32[16,16,128]{2,1,0:T(8,128)} custom-call(f32[12,2,8,128]{3,2,1,0:T(8,128)S(1)} %get-tuple-element.21.rim_ref, f32[3,8,128]{2,1,0:T(8,128)S(1)} %collective-permute-done.2.first_ref, f32[3,8,128]{2,1,0:T(8,128)S(1)} %collective-permute-done.3.second_ref, f32[2,8,128]{2,1,0:T(8,128)S(1)} %get-tuple-element.24.rate_ref, ...), custom_call_target="tpu_custom_call" | custom-call | flops 20000000 | bytes 500000 | tf_op jit(solution)/shard_map/rim/pallas_call | solution.py:455
Async XLA Ops:
  0.0 13.1 %collective-permute-start = (f32[16,16,128]{2,1,0:T(8,128)}, f32[16,16,128]{2,1,0:T(8,128)S(1)}, u32[]{:S(2)}, u32[]{:S(2)}) collective-permute-start(f32[16,16,128]{2,1,0:T(8,128)} %noisy_ref.1), channel_id=1, source_target_pairs={{0,4},{8,12},{16,20},{24,28},{32,36},{40,44},{48,52},{56,60},{64,6... | collective-permute-start | bytes 393224 | tf_op jit(solution)/shard_map/ppermute | solution.py:423
  1.2 11.9 %collective-permute-start.1 = (f32[16,16,128]{2,1,0:T(8,128)}, f32[16,16,128]{2,1,0:T(8,128)S(1)}, u32[]{:S(2)}, u32[]{:S(2)}) collective-permute-start(f32[16,16,128]{2,1,0:T(8,128)} %noisy_ref.1), channel_id=1, source_target_pairs={{4,8},{12,16},{20,24},{28,32},{36,40},{44,48},{52,56},{60,64},{68,... | collective-permute-start | bytes 393224 | tf_op jit(solution)/shard_map/ppermute | solution.py:423
  7.1 0.9 %copy-start = (f32[16,16,128]{2,1,0:T(8,128)S(1)}, f32[16,16,128]{2,1,0:T(8,128)}, u32[]{:S(2)}) copy-start(f32[16,16,128]{2,1,0:T(8,128)} %noisy_ref.1) | copy-start | bytes 393220
  13.3 9.5 %collective-permute-start.2 = (f32[3,8,128]{2,1,0:T(8,128)S(1)}, f32[3,8,128]{2,1,0:T(8,128)S(1)}, u32[]{:S(2)}, u32[]{:S(2)}) collective-permute-start(f32[3,8,128]{2,1,0:T(8,128)S(1)} %get-tuple-element.22), channel_id=1, source_target_pairs={{0,1},{2,3},{1,0},{3,2},{4,5},{6,7},{5,4},{7,6},{8,9},{10,11},{9,8... | collective-permute-start | bytes 36872 | tf_op jit(solution)/shard_map/ppermute | solution.py:423
  14.6 8.2 %collective-permute-start.3 = (f32[3,8,128]{2,1,0:T(8,128)S(1)}, f32[3,8,128]{2,1,0:T(8,128)S(1)}, u32[]{:S(2)}, u32[]{:S(2)}) collective-permute-start(f32[3,8,128]{2,1,0:T(8,128)S(1)} %get-tuple-element.23), channel_id=1, source_target_pairs={{1,2},{2,1},{5,6},{6,5},{9,10},{10,9},{13,14},{14,13},{17,18},{18,... | collective-permute-start | bytes 36872 | tf_op jit(solution)/shard_map/ppermute | solution.py:423

commit v3 on v2

--- a/solution.py
+++ b/solution.py
@@ -10,6 +10,7 @@
 F = jnp.float32
 B = jnp.bfloat16
 HALO = 4
+SPLIT = 3
 
 
 def lanes():
@@ -117,11 +118,11 @@
     band = jnp.where(abs(line - column) <= 2, 1.0, 0.0).astype(B)
     for sy in range(5):
         place = {}
+        base, todo, parts = 0, [], []
         for shift_z in range(3):
-            base, todo, parts = 0, [], []
             for n, shift_x in enumerate(offsets(shift_z, sy)):
                 slot = 0
-                for rows in segments(shift_x):
+                for rows in segments(shift_x, sy):
                     patch_sums(
                         rows,
                         row,
@@ -129,11 +130,12 @@
                         lambda x, parity: below(sy, x + shift_x, (shift_z - 1) * (1 + parity)) if shift_z else 0.0,
                         parts,
                     )
-                    todo.append((shift_x, rows, base, n, slot))
+                    todo.append((shift_z, shift_x, rows, base, n, slot))
                     base += 16 * rows[1]
                     slot += rows[1]
+        if parts:
             sums = jnp.dot(jnp.concatenate(parts, 0), band, preferred_element_type=F)
-            for shift_x, rows, at, n, slot in todo:
+            for shift_z, shift_x, rows, at, n, slot in todo:
                 for j in range(rows[1]):
                     x = rows[0] + j
                     for parity in range(2):
@@ -198,17 +200,21 @@
     ]
 
 
-def inner_segments(shift_x):
+def inner_segments(shift_x, sy):
+    if sy >= SPLIT:
+        return ()
     return ((2 + max(0, -shift_x), 12 - abs(shift_x)),)
 
 
-def outer_segments(shift_x):
+def outer_segments(shift_x, sy):
+    if sy >= SPLIT:
+        return ((-max(0, shift_x), 16 + abs(shift_x)),)
     many = 2 + abs(shift_x)
     return ((-max(0, shift_x), many), (14 - max(0, shift_x), many))
 
 
 def whole_segments(nx):
-    return lambda shift_x: ((-max(0, shift_x), nx + abs(shift_x)),)
+    return lambda shift_x, sy: ((-max(0, shift_x), nx + abs(shift_x)),)
 
 
 def to_strips(value, chunk):
@@ -315,10 +321,10 @@
         return moved_row(far, sy, x + HALO if x < 0 else x - 12, shift_z, parity)
 
     def taken(sy, x, j):
-        return below[sy, x + 2 if x < 6 else x - 2, j]
+        return below[sy, x + 2, j]
 
     fill_copies(far, steps, 8, lambda x, parity: row(x - HALO if x < HALO else x + 12, parity))
-    fill_below(below, [*range(-2, 6), *range(10, 18)], row)
+    fill_below(below, range(-2, 18), row)
     one = jnp.ones((8, 128), F)
     accumulate(
         16,
@@ -427,8 +433,8 @@
     V = pltpu.VMEM
     row4, row12, row16, three = shape(4, 2, 8, 128), shape(12, 2, 8, 128), shape(16, 2, 8, 128), shape(3, 8, 128)
     rates = ((-math.log2(math.e) / 125.0) / strength).reshape(1, 16)
+    other = swapped(noisy, "gx", 1)
     pair = swapped(noisy, "gx", 0)
-    other = swapped(noisy, "gx", 1)
     own, rate, copies, inner_w, inner_t, rim, to_left, to_right = call(
         inner_kernel,
         "inner",
@@ -440,14 +446,14 @@
     low, high, rim, first, second = call(join_kernel, "join", (row4, row4, row12, three, three), [], 4)(
         pair, other, rim, to_left, to_right
     )
+    second = swapped(second, "gy", 1)
     first = swapped(first, "gy", 0)
-    second = swapped(second, "gy", 1)
     mid = call(
         outer_kernel,
         "outer",
         row16,
-        [V((5, 8, 5, 8, 128), F), V((8, 2, 16, 128), F), V((5, 16, 3, 8, 128), F)]
-        + work(16, 8)
+        [V((5, 8, 5, 8, 128), F), V((8, 2, 16, 128), F), V((5, 20, 3, 8, 128), F)]
+        + work(16, 18)
         + [V((16, 2, 8, 128), F)] * 2,
         20,
         40_000_000,

time: 26.1 us -> 26 us (level)
  Pallas kernels: 11.4 us -> 11.1 us
    pallas_call x1, Pallas kernels: 5.06 us -> 3.04 us  [per_device(): call(inner_kernel, 'inner', (row16, shape(2, 8, 128), shape(5, 16, 5, 8,...]
    pallas_call x1, Pallas kernels: 3.05 us -> 4.81 us  [per_device(): call(outer_kernel, 'outer', row16, [V((5, 8, 5, 8, 128), F), V((8, 2, 16,...]
  transfers between devices with their start and end apart: 4 -> 4, of which waited for: 0 -> 0; matrix products, arithmetic and copies ran while one was open for 3% -> 3% of each run, Pallas kernels for 31% -> 30%
where the time goes in v3:
time: 26 us; the launch traced here: 25.8 us
  starting transfers between devices  13.1 us (50%)
  Pallas kernels  11.1 us (43%)
  local copies, waits for them, and re-layouts  0.91 us (4%)
  other arithmetic  0.66 us (3%)
    ppermute x4, starting transfers between devices, swapped(): return lax.ppermute(value, axis, pairs + [(b, a) for a, b in pairs])  13.1 us
    pallas_call x1, Pallas kernels, per_device(): call(outer_kernel, 'outer', row16, [V((5, 8, 5, 8, 128), F), V((8, 2, 16,...  4.81 us
    pallas_call x1, Pallas kernels, per_device(): call(rim_kernel, 'rim', shape(16, 16, 128), [V((12, 2, 8, 128), F), V((5,...  3.06 us
    pallas_call x1, Pallas kernels, per_device(): call(inner_kernel, 'inner', (row16, shape(2, 8, 128), shape(5, 16, 5, 8,...  3.04 us
    unnamed x2, local copies, waits for them, and re-layouts  0.91 us
    reshape x1, other arithmetic, per_device(): rates = (-math.log2(math.e) / 125.0 / strength).reshape(1, 16)  0.66 us
  transfers between devices with their start and end apart: 4, of which 0 were waited for; matrix products, arithmetic and copies ran while one was open for 3% of the time, Pallas kernels for 30%

profile of v3, /device:TPU:25, one launch (start us, length us, event | category | flops | bytes accessed | tf_op | source)
XLA Modules:
  0.0 25.8 jit_solution(18086192962147227306)
XLA Ops:
  0.0 1.2 %collective-permute-start = (f32[16,16,128]{2,1,0:T(8,128)}, f32[16,16,128]{2,1,0:T(8,128)S(1)}, u32[]{:S(2)}, u32[]{:S(2)}) collective-permute-start(f32[16,16,128]{2,1,0:T(8,128)} %noisy_ref.1), channel_id=1, source_target_pairs={{0,4},{8,12},{16,20},{24,28},{32,36},{40,44},{48,52},{56,60},{64,6... | collective-permute-start | bytes 393224 | tf_op jit(solution)/shard_map/ppermute | solution.py:429
  1.2 5.2 %collective-permute-start.1 = (f32[16,16,128]{2,1,0:T(8,128)}, f32[16,16,128]{2,1,0:T(8,128)S(1)}, u32[]{:S(2)}, u32[]{:S(2)}) collective-permute-start(f32[16,16,128]{2,1,0:T(8,128)} %noisy_ref.1), channel_id=1, source_target_pairs={{4,8},{12,16},{20,24},{28,32},{36,40},{44,48},{52,56},{60,64},{68,... | collective-permute-start | bytes 393224 | tf_op jit(solution)/shard_map/ppermute | solution.py:429
  6.5 0.7 %divide_bitcast_fusion.slices_ref = f32[1,16]{1,0:T(1,128)S(1)} fusion(f32[16]{0:T(128)} %param.3), kind=kLoop, calls=%fused_computation | loop fusion | flops 16 | bytes 128 | tf_op jit(solution)/shard_map/reshape | solution.py:435
  7.1 0.0 copy-start
  7.1 0.9 %copy-done = f32[16,16,128]{2,1,0:T(8,128)S(1)} copy-done((f32[16,16,128]{2,1,0:T(8,128)S(1)}, f32[16,16,128]{2,1,0:T(8,128)}, u32[]{:S(2)}) %copy-start) | copy-done | bytes 131096
  8.0 3.0 %inner.1 = (f32[16,2,8,128]{3,2,1,0:T(8,128)S(1)}, f32[2,8,128]{2,1,0:T(8,128)S(1)}, f32[5,16,5,8,128]{4,3,2,1,0:T(8,128)S(1)}, f32[16,2,8,128]{3,2,1,0:T(8,128)...) custom-call(f32[16,16,128]{2,1,0:T(8,128)S(1)} %copy-done, ...), custom_call_target="tpu_custom_call" | custom-call | flops 60000000 | bytes 500000 | tf_op jit(solution)/shard_map/inner/pallas_call | solution.py:438
  11.1 0.0 collective-permute-done.pair_ref
  11.1 0.0 collective-permute-done.1.next_ref
  11.1 0.2 join.1
  11.3 1.3 %collective-permute-start.2 = (f32[3,8,128]{2,1,0:T(8,128)S(1)}, f32[3,8,128]{2,1,0:T(8,128)S(1)}, u32[]{:S(2)}, u32[]{:S(2)}) collective-permute-start(f32[3,8,128]{2,1,0:T(8,128)S(1)} %get-tuple-element.22), channel_id=1, source_target_pairs={{0,1},{2,3},{1,0},{3,2},{4,5},{6,7},{5,4},{7,6},{8,9},{10,11},{9,8... | collective-permute-start | bytes 36872 | tf_op jit(solution)/shard_map/ppermute | solution.py:429
  12.6 5.3 %collective-permute-start.3 = (f32[3,8,128]{2,1,0:T(8,128)S(1)}, f32[3,8,128]{2,1,0:T(8,128)S(1)}, u32[]{:S(2)}, u32[]{:S(2)}) collective-permute-start(f32[3,8,128]{2,1,0:T(8,128)S(1)} %get-tuple-element.23), channel_id=1, source_target_pairs={{1,2},{2,1},{5,6},{6,5},{9,10},{10,9},{13,14},{14,13},{17,18},{18,... | collective-permute-start | bytes 36872 | tf_op jit(solution)/shard_map/ppermute | solution.py:429
  17.9 4.8 %outer.1.mid_ref = f32[16,2,8,128]{3,2,1,0:T(8,128)S(1)} custom-call(f32[16,2,8,128]{3,2,1,0:T(8,128)S(1)} %get-tuple-element.25.own_ref, f32[4,2,8,128]{3,2,1,0:T(8,128)S(1)} %get-tuple-element.26.low_ref, f32[4,2,8,128]{3,2,1,0:T(8,128)S(1)} %get-tuple-element.27.high_ref, f32[5,16,5,8,128]{4,3,2,1,0:T(8,128)S(1)} %get-tuple-element.28.copies, ...), custom_call_target="tpu_custom_call" | custom-call | flops 40000000 | bytes 500000 | tf_op jit(solution)/shard_map/outer/pallas_call | solution.py:451
  22.7 0.0 collective-permute-done.2.first_ref
  22.7 0.0 collective-permute-done.3.second_ref
  22.8 3.1 %rim.1 = f32[16,16,128]{2,1,0:T(8,128)} custom-call(f32[12,2,8,128]{3,2,1,0:T(8,128)S(1)} %get-tuple-element.21.rim_ref, f32[3,8,128]{2,1,0:T(8,128)S(1)} %collective-permute-done.2.first_ref, f32[3,8,128]{2,1,0:T(8,128)S(1)} %collective-permute-done.3.second_ref, f32[2,8,128]{2,1,0:T(8,128)S(1)} %get-tuple-element.24.rate_ref, ...), custom_call_target="tpu_custom_call" | custom-call | flops 20000000 | bytes 500000 | tf_op jit(solution)/shard_map/rim/pallas_call | solution.py:461
Async XLA Ops:
  0.0 11.1 %collective-permute-start = (f32[16,16,128]{2,1,0:T(8,128)}, f32[16,16,128]{2,1,0:T(8,128)S(1)}, u32[]{:S(2)}, u32[]{:S(2)}) collective-permute-start(f32[16,16,128]{2,1,0:T(8,128)} %noisy_ref.1), channel_id=1, source_target_pairs={{0,4},{8,12},{16,20},{24,28},{32,36},{40,44},{48,52},{56,60},{64,6... | collective-permute-start | bytes 393224 | tf_op jit(solution)/shard_map/ppermute | solution.py:429
  1.2 9.9 %collective-permute-start.1 = (f32[16,16,128]{2,1,0:T(8,128)}, f32[16,16,128]{2,1,0:T(8,128)S(1)}, u32[]{:S(2)}, u32[]{:S(2)}) collective-permute-start(f32[16,16,128]{2,1,0:T(8,128)} %noisy_ref.1), channel_id=1, source_target_pairs={{4,8},{12,16},{20,24},{28,32},{36,40},{44,48},{52,56},{60,64},{68,... | collective-permute-start | bytes 393224 | tf_op jit(solution)/shard_map/ppermute | solution.py:429
  7.1 0.9 %copy-start = (f32[16,16,128]{2,1,0:T(8,128)S(1)}, f32[16,16,128]{2,1,0:T(8,128)}, u32[]{:S(2)}) copy-start(f32[16,16,128]{2,1,0:T(8,128)} %noisy_ref.1) | copy-start | bytes 393220
  11.3 11.4 %collective-permute-start.2 = (f32[3,8,128]{2,1,0:T(8,128)S(1)}, f32[3,8,128]{2,1,0:T(8,128)S(1)}, u32[]{:S(2)}, u32[]{:S(2)}) collective-permute-start(f32[3,8,128]{2,1,0:T(8,128)S(1)} %get-tuple-element.22), channel_id=1, source_target_pairs={{0,1},{2,3},{1,0},{3,2},{4,5},{6,7},{5,4},{7,6},{8,9},{10,11},{9,8... | collective-permute-start | bytes 36872 | tf_op jit(solution)/shard_map/ppermute | solution.py:429
  12.6 10.1 %collective-permute-start.3 = (f32[3,8,128]{2,1,0:T(8,128)S(1)}, f32[3,8,128]{2,1,0:T(8,128)S(1)}, u32[]{:S(2)}, u32[]{:S(2)}) collective-permute-start(f32[3,8,128]{2,1,0:T(8,128)S(1)} %get-tuple-element.23), channel_id=1, source_target_pairs={{1,2},{2,1},{5,6},{6,5},{9,10},{10,9},{13,14},{14,13},{17,18},{18,... | collective-permute-start | bytes 36872 | tf_op jit(solution)/shard_map/ppermute | solution.py:429

commit v4 on v3

--- a/solution.py
+++ b/solution.py
@@ -10,7 +10,7 @@
 F = jnp.float32
 B = jnp.bfloat16
 HALO = 4
-SPLIT = 3
+SPLIT = 4
 
 
 def lanes():
@@ -274,7 +274,7 @@
     )
 
 
-def join_kernel(pair_ref, next_ref, rim_ref, left_ref, right_ref, low_ref, high_ref, rim_out, first_out, second_out):
+def join_kernel(next_ref, pair_ref, rim_ref, left_ref, right_ref, low_ref, high_ref, rim_out, first_out, second_out):
     odd = flag("odd_x") > 0.5
     pair, other = pair_ref.reshape(256, 128), next_ref.reshape(256, 128)
     for x in range(HALO):
@@ -343,7 +343,7 @@
             mid_ref[x, parity] = scratch[-2][x, parity] / scratch[-1][x, parity]
 
 
-def rim_kernel(rim_ref, first_ref, second_ref, rate_ref, mid_ref, out_ref, rows, copies, steps, below, column_mask, *scratch):
+def rim_kernel(rim_ref, second_ref, first_ref, rate_ref, mid_ref, out_ref, rows, copies, steps, below, column_mask, *scratch):
     lane = lanes()
     spot = lane % 32
     odd = flag("odd_y") > 0.5
@@ -444,7 +444,7 @@
         60_000_000,
     )(noisy, rates)
     low, high, rim, first, second = call(join_kernel, "join", (row4, row4, row12, three, three), [], 4)(
-        pair, other, rim, to_left, to_right
+        other, pair, rim, to_left, to_right
     )
     second = swapped(second, "gy", 1)
     first = swapped(first, "gy", 0)
@@ -467,7 +467,7 @@
         + [V((4, 2, 8, 128), F)] * 2,
         20,
         20_000_000,
-    )(rim, first, second, rate, mid)
+    )(rim, second, first, rate, mid)
 
 
 def solution(mesh):

time: 26 us -> 25.7 us (0.988)
  the two profiles are of different devices: /device:TPU:25 before, /device:TPU:27 now
where the time goes in v4:
time: 25.7 us; the launch traced here: 25.5 us
  starting transfers between devices  12.7 us (49%)
  Pallas kernels  11.2 us (44%)
  local copies, waits for them, and re-layouts  0.91 us (4%)
  other arithmetic  0.66 us (3%)
    ppermute x4, starting transfers between devices, swapped(): return lax.ppermute(value, axis, pairs + [(b, a) for a, b in pairs])  12.7 us
    pallas_call x1, Pallas kernels, per_device(): call(inner_kernel, 'inner', (row16, shape(2, 8, 128), shape(5, 16, 5, 8,...  4.07 us
    pallas_call x1, Pallas kernels, per_device(): call(outer_kernel, 'outer', row16, [V((5, 8, 5, 8, 128), F), V((8, 2, 16,...  3.89 us
    pallas_call x1, Pallas kernels, per_device(): call(rim_kernel, 'rim', shape(16, 16, 128), [V((12, 2, 8, 128), F), V((5,...  3.06 us
    unnamed x2, local copies, waits for them, and re-layouts  0.91 us
    reshape x1, other arithmetic, per_device(): rates = (-math.log2(math.e) / 125.0 / strength).reshape(1, 16)  0.66 us
  transfers between devices with their start and end apart: 4, of which 0 were waited for; matrix products, arithmetic and copies ran while one was open for 3% of the time, Pallas kernels for 31%

profile of v4, /device:TPU:27, one launch (start us, length us, event | category | flops | bytes accessed | tf_op | source)
XLA Modules:
  0.0 25.5 jit_solution(13640009417262809974)
XLA Ops:
  0.0 3.1 %collective-permute-start = (f32[16,16,128]{2,1,0:T(8,128)}, f32[16,16,128]{2,1,0:T(8,128)S(1)}, u32[]{:S(2)}, u32[]{:S(2)}) collective-permute-start(f32[16,16,128]{2,1,0:T(8,128)} %noisy_ref.1), channel_id=1, source_target_pairs={{4,8},{12,16},{20,24},{28,32},{36,40},{44,48},{52,56},{60,64},{68,... | collective-permute-start | bytes 393224 | tf_op jit(solution)/shard_map/ppermute | solution.py:429
  3.1 3.1 %collective-permute-start.1 = (f32[16,16,128]{2,1,0:T(8,128)}, f32[16,16,128]{2,1,0:T(8,128)S(1)}, u32[]{:S(2)}, u32[]{:S(2)}) collective-permute-start(f32[16,16,128]{2,1,0:T(8,128)} %noisy_ref.1), channel_id=1, source_target_pairs={{0,4},{8,12},{16,20},{24,28},{32,36},{40,44},{48,52},{56,60},{64,6... | collective-permute-start | bytes 393224 | tf_op jit(solution)/shard_map/ppermute | solution.py:429
  6.3 0.7 %divide_bitcast_fusion.slices_ref = f32[1,16]{1,0:T(1,128)S(1)} fusion(f32[16]{0:T(128)} %param.3), kind=kLoop, calls=%fused_computation | loop fusion | flops 16 | bytes 128 | tf_op jit(solution)/shard_map/reshape | solution.py:435
  6.9 0.0 copy-start
  6.9 0.9 %copy-done = f32[16,16,128]{2,1,0:T(8,128)S(1)} copy-done((f32[16,16,128]{2,1,0:T(8,128)S(1)}, f32[16,16,128]{2,1,0:T(8,128)}, u32[]{:S(2)}) %copy-start) | copy-done | bytes 131096
  7.8 4.1 %inner.1 = (f32[16,2,8,128]{3,2,1,0:T(8,128)S(1)}, f32[2,8,128]{2,1,0:T(8,128)S(1)}, f32[5,16,5,8,128]{4,3,2,1,0:T(8,128)S(1)}, f32[16,2,8,128]{3,2,1,0:T(8,128)...) custom-call(f32[16,16,128]{2,1,0:T(8,128)S(1)} %copy-done, ...), custom_call_target="tpu_custom_call" | custom-call | flops 60000000 | bytes 500000 | tf_op jit(solution)/shard_map/inner/pallas_call | solution.py:438
  11.9 0.0 collective-permute-done.next_ref
  11.9 0.0 collective-permute-done.1.pair_ref
  11.9 0.2 join.1
  12.1 6.3 %collective-permute-start.2 = (f32[3,8,128]{2,1,0:T(8,128)S(1)}, f32[3,8,128]{2,1,0:T(8,128)S(1)}, u32[]{:S(2)}, u32[]{:S(2)}) collective-permute-start(f32[3,8,128]{2,1,0:T(8,128)S(1)} %get-tuple-element.22), channel_id=1, source_target_pairs={{1,2},{2,1},{5,6},{6,5},{9,10},{10,9},{13,14},{14,13},{17,18},{18,... | collective-permute-start | bytes 36872 | tf_op jit(solution)/shard_map/ppermute | solution.py:429
  18.4 0.1 collective-permute-start.3
  18.5 3.9 %outer.1.mid_ref = f32[16,2,8,128]{3,2,1,0:T(8,128)S(1)} custom-call(f32[16,2,8,128]{3,2,1,0:T(8,128)S(1)} %get-tuple-element.25.own_ref, f32[4,2,8,128]{3,2,1,0:T(8,128)S(1)} %get-tuple-element.26.low_ref, f32[4,2,8,128]{3,2,1,0:T(8,128)S(1)} %get-tuple-element.27.high_ref, f32[5,16,5,8,128]{4,3,2,1,0:T(8,128)S(1)} %get-tuple-element.28.copies, ...), custom_call_target="tpu_custom_call" | custom-call | flops 40000000 | bytes 500000 | tf_op jit(solution)/shard_map/outer/pallas_call | solution.py:451
  22.4 0.0 collective-permute-done.2.second_ref
  22.4 0.0 collective-permute-done.3.first_ref
  22.5 3.1 %rim.1 = f32[16,16,128]{2,1,0:T(8,128)} custom-call(f32[12,2,8,128]{3,2,1,0:T(8,128)S(1)} %get-tuple-element.21.rim_ref, f32[3,8,128]{2,1,0:T(8,128)S(1)} %collective-permute-done.2.second_ref, f32[3,8,128]{2,1,0:T(8,128)S(1)} %collective-permute-done.3.first_ref, f32[2,8,128]{2,1,0:T(8,128)S(1)} %get-tuple-element.24.rate_ref, ...), custom_call_target="tpu_custom_call" | custom-call | flops 20000000 | bytes 500000 | tf_op jit(solution)/shard_map/rim/pallas_call | solution.py:461
Async XLA Ops:
  0.0 11.9 %collective-permute-start = (f32[16,16,128]{2,1,0:T(8,128)}, f32[16,16,128]{2,1,0:T(8,128)S(1)}, u32[]{:S(2)}, u32[]{:S(2)}) collective-permute-start(f32[16,16,128]{2,1,0:T(8,128)} %noisy_ref.1), channel_id=1, source_target_pairs={{4,8},{12,16},{20,24},{28,32},{36,40},{44,48},{52,56},{60,64},{68,... | collective-permute-start | bytes 393224 | tf_op jit(solution)/shard_map/ppermute | solution.py:429
  3.1 8.8 %collective-permute-start.1 = (f32[16,16,128]{2,1,0:T(8,128)}, f32[16,16,128]{2,1,0:T(8,128)S(1)}, u32[]{:S(2)}, u32[]{:S(2)}) collective-permute-start(f32[16,16,128]{2,1,0:T(8,128)} %noisy_ref.1), channel_id=1, source_target_pairs={{0,4},{8,12},{16,20},{24,28},{32,36},{40,44},{48,52},{56,60},{64,6... | collective-permute-start | bytes 393224 | tf_op jit(solution)/shard_map/ppermute | solution.py:429
  6.9 0.9 %copy-start = (f32[16,16,128]{2,1,0:T(8,128)S(1)}, f32[16,16,128]{2,1,0:T(8,128)}, u32[]{:S(2)}) copy-start(f32[16,16,128]{2,1,0:T(8,128)} %noisy_ref.1) | copy-start | bytes 393220
  12.1 10.3 %collective-permute-start.2 = (f32[3,8,128]{2,1,0:T(8,128)S(1)}, f32[3,8,128]{2,1,0:T(8,128)S(1)}, u32[]{:S(2)}, u32[]{:S(2)}) collective-permute-start(f32[3,8,128]{2,1,0:T(8,128)S(1)} %get-tuple-element.22), channel_id=1, source_target_pairs={{1,2},{2,1},{5,6},{6,5},{9,10},{10,9},{13,14},{14,13},{17,18},{18,... | collective-permute-start | bytes 36872 | tf_op jit(solution)/shard_map/ppermute | solution.py:429
  18.4 4.0 %collective-permute-start.3 = (f32[3,8,128]{2,1,0:T(8,128)S(1)}, f32[3,8,128]{2,1,0:T(8,128)S(1)}, u32[]{:S(2)}, u32[]{:S(2)}) collective-permute-start(f32[3,8,128]{2,1,0:T(8,128)S(1)} %get-tuple-element.23), channel_id=1, source_target_pairs={{0,1},{2,3},{1,0},{3,2},{4,5},{6,7},{5,4},{7,6},{8,9},{10,11},{9,8... | collective-permute-start | bytes 36872 | tf_op jit(solution)/shard_map/ppermute | solution.py:429

commit v5 on v4

--- a/solution.py
+++ b/solution.py
@@ -274,7 +274,10 @@
     )
 
 
-def join_kernel(next_ref, pair_ref, rim_ref, left_ref, right_ref, low_ref, high_ref, rim_out, first_out, second_out):
+def join_kernel(
+    next_ref, pair_ref, rim_ref, left_ref, right_ref, own_ref, copies, rate_ref, inner_w, inner_t,
+    low_ref, high_ref, rim_out, first_out, second_out, mid_ref, *scratch,
+):
     odd = flag("odd_x") > 0.5
     pair, other = pair_ref.reshape(256, 128), next_ref.reshape(256, 128)
     for x in range(HALO):
@@ -308,8 +311,28 @@
         first_out[group] = jnp.where(odd, left, right)
         second_out[group] = jnp.where(odd, right, left)
 
-
-def outer_kernel(own_ref, low_ref, high_ref, copies, rate_ref, inner_w, inner_t, mid_ref, far, steps, below, *scratch):
+    @pl.when(starts_early())
+    def _():
+        outer_rows(own_ref, low_ref, high_ref, copies, rate_ref, inner_w, inner_t, mid_ref, *scratch)
+
+
+def starts_early():
+    return 2 * lax.axis_index("gy") < lax.axis_size("gy")
+
+
+def outer_kernel(own_ref, low_ref, high_ref, copies, rate_ref, inner_w, inner_t, done_ref, mid_ref, *scratch):
+    early = starts_early()
+
+    @pl.when(early)
+    def _():
+        mid_ref[...] = done_ref[...]
+
+    @pl.when(jnp.logical_not(early))
+    def _():
+        outer_rows(own_ref, low_ref, high_ref, copies, rate_ref, inner_w, inner_t, mid_ref, *scratch)
+
+
+def outer_rows(own_ref, low_ref, high_ref, copies, rate_ref, inner_w, inner_t, mid_ref, far, steps, below, *scratch):
     def row(x, parity):
         if x < 0:
             return low_ref[x + HALO, parity]
@@ -421,7 +444,7 @@
     )
 
 
-INPUTS = {"inner": 2, "join": 5, "outer": 7, "rim": 5}
+INPUTS = {"inner": 2, "join": 10, "outer": 8, "rim": 5}
 
 
 def swapped(value, axis, first):
@@ -443,21 +466,19 @@
         20,
         60_000_000,
     )(noisy, rates)
-    low, high, rim, first, second = call(join_kernel, "join", (row4, row4, row12, three, three), [], 4)(
-        other, pair, rim, to_left, to_right
-    )
+    outer_scratch = (
+        [V((5, 8, 5, 8, 128), F), V((8, 2, 16, 128), F), V((5, 20, 3, 8, 128), F)]
+        + work(16, 18)
+        + [V((16, 2, 8, 128), F)] * 2
+    )
+    low, high, rim, first, second, done = call(
+        join_kernel, "join", (row4, row4, row12, three, three, row16), outer_scratch, 20
+    )(other, pair, rim, to_left, to_right, own, copies, rate, inner_w, inner_t)
     second = swapped(second, "gy", 1)
     first = swapped(first, "gy", 0)
-    mid = call(
-        outer_kernel,
-        "outer",
-        row16,
-        [V((5, 8, 5, 8, 128), F), V((8, 2, 16, 128), F), V((5, 20, 3, 8, 128), F)]
-        + work(16, 18)
-        + [V((16, 2, 8, 128), F)] * 2,
-        20,
-        40_000_000,
-    )(own, low, high, copies, rate, inner_w, inner_t)
+    mid = call(outer_kernel, "outer", row16, outer_scratch, 20, 40_000_000)(
+        own, low, high, copies, rate, inner_w, inner_t, done
+    )
     return call(
         rim_kernel,
         "rim",

time: 25.7 us -> 25.7 us (level)
  the two profiles are of different devices: /device:TPU:27 before, /device:TPU:25 now
where the time goes in v5:
time: 25.7 us; the launch traced here: 25.3 us
  Pallas kernels  11.4 us (44%)
  starting transfers between devices  8.24 us (32%)
  waiting for transfers between devices  4.06 us (16%)
  local copies, waits for them, and re-layouts  0.91 us (4%)
  other arithmetic  0.66 us (3%)
    ppermute x4, starting transfers between devices, swapped(): return lax.ppermute(value, axis, pairs + [(b, a) for a, b in pairs])  8.24 us
    pallas_call x1, Pallas kernels, per_device(): call(join_kernel, 'join', (row4, row4, row12, three, three, row16), outer...  4.07 us
    ppermute x4, waiting for transfers between devices, swapped(): return lax.ppermute(value, axis, pairs + [(b, a) for a, b in pairs])  4.06 us
    pallas_call x1, Pallas kernels, per_device(): call(inner_kernel, 'inner', (row16, shape(2, 8, 128), shape(5, 16, 5, 8,...  4.05 us
    pallas_call x1, Pallas kernels, per_device(): call(rim_kernel, 'rim', shape(16, 16, 128), [V((12, 2, 8, 128), F), V((5,...  3.05 us
    unnamed x2, local copies, waits for them, and re-layouts  0.91 us
    reshape x1, other arithmetic, per_device(): rates = (-math.log2(math.e) / 125.0 / strength).reshape(1, 16)  0.66 us
  transfers between devices with their start and end apart: 4, of which 1 were waited for; matrix products, arithmetic and copies ran while one was open for 3% of the time, Pallas kernels for 17%

profile of v5, /device:TPU:25, one launch (start us, length us, event | category | flops | bytes accessed | tf_op | source)
XLA Modules:
  0.0 25.3 jit_solution(5669871169456136469)
XLA Ops:
  0.0 5.9 %collective-permute-start = (f32[16,16,128]{2,1,0:T(8,128)}, f32[16,16,128]{2,1,0:T(8,128)S(1)}, u32[]{:S(2)}, u32[]{:S(2)}) collective-permute-start(f32[16,16,128]{2,1,0:T(8,128)} %noisy_ref.1), channel_id=1, source_target_pairs={{4,8},{12,16},{20,24},{28,32},{36,40},{44,48},{52,56},{60,64},{68,... | collective-permute-start | bytes 393224 | tf_op jit(solution)/shard_map/ppermute | solution.py:452
  5.9 0.1 collective-permute-start.1
  6.0 0.7 %divide_bitcast_fusion.slices_ref = f32[1,16]{1,0:T(1,128)S(1)} fusion(f32[16]{0:T(128)} %param.3), kind=kLoop, calls=%fused_computation | loop fusion | flops 16 | bytes 128 | tf_op jit(solution)/shard_map/reshape | solution.py:458
  6.7 0.0 copy-start
  6.7 0.9 %copy-done = f32[16,16,128]{2,1,0:T(8,128)S(1)} copy-done((f32[16,16,128]{2,1,0:T(8,128)S(1)}, f32[16,16,128]{2,1,0:T(8,128)}, u32[]{:S(2)}) %copy-start) | copy-done | bytes 131096
  7.6 4.1 %inner.1 = (f32[16,2,8,128]{3,2,1,0:T(8,128)S(1)}, f32[2,8,128]{2,1,0:T(8,128)S(1)}, f32[5,16,5,8,128]{4,3,2,1,0:T(8,128)S(1)}, f32[16,2,8,128]{3,2,1,0:T(8,128)...) custom-call(f32[16,16,128]{2,1,0:T(8,128)S(1)} %copy-done, ...), custom_call_target="tpu_custom_call" | custom-call | flops 60000000 | bytes 500000 | tf_op jit(solution)/shard_map/inner/pallas_call | solution.py:461
  11.6 0.0 collective-permute-done.next_ref
  11.7 0.0 collective-permute-done.1.pair_ref
  11.7 4.1 %join.1 = (f32[4,2,8,128]{3,2,1,0:T(8,128)S(1)}, f32[4,2,8,128]{3,2,1,0:T(8,128)S(1)}, f32[12,2,8,128]{3,2,1,0:T(8,128)S(1)}, f32[3,8,128]{2,1,0:T(8,128)S(1)}, ...) custom-call(f32[16,16,128]{2,1,0:T(8,128)S(1)} %collective-permute-done.next_ref, ...), custom_call_target="tpu_custom_call" | custom-call | bytes 500000 | tf_op jit(solution)/shard_map/join/pallas_call | solution.py:474
  15.7 2.2 %collective-permute-start.2 = (f32[3,8,128]{2,1,0:T(8,128)S(1)}, f32[3,8,128]{2,1,0:T(8,128)S(1)}, u32[]{:S(2)}, u32[]{:S(2)}) collective-permute-start(f32[3,8,128]{2,1,0:T(8,128)S(1)} %get-tuple-element.28), channel_id=1, source_target_pairs={{1,2},{2,1},{5,6},{6,5},{9,10},{10,9},{13,14},{14,13},{17,18},{18,... | collective-permute-start | bytes 36872 | tf_op jit(solution)/shard_map/ppermute | solution.py:452
  17.9 0.1 collective-permute-start.3
  18.0 0.2 outer.1.mid_ref
  18.2 4.0 %collective-permute-done.2.second_ref = f32[3,8,128]{2,1,0:T(8,128)S(1)} collective-permute-done((f32[3,8,128]{2,1,0:T(8,128)S(1)}, f32[3,8,128]{2,1,0:T(8,128)S(1)}, u32[]{:S(2)}, u32[]{:S(2)}) %collective-permute-start.2) | collective-permute-done | bytes 12320 | tf_op jit(solution)/shard_map/ppermute | solution.py:452
  22.3 0.0 collective-permute-done.3.first_ref
  22.3 3.1 %rim.1 = f32[16,16,128]{2,1,0:T(8,128)} custom-call(f32[12,2,8,128]{3,2,1,0:T(8,128)S(1)} %get-tuple-element.27.rim_ref, f32[3,8,128]{2,1,0:T(8,128)S(1)} %collective-permute-done.2.second_ref, f32[3,8,128]{2,1,0:T(8,128)S(1)} %collective-permute-done.3.first_ref, f32[2,8,128]{2,1,0:T(8,128)S(1)} %get-tuple-element.24.rate_ref, ...), custom_call_target="tpu_custom_call" | custom-call | flops 20000000 | bytes 500000 | tf_op jit(solution)/shard_map/rim/pallas_call | solution.py:482
Async XLA Ops:
  0.0 11.6 %collective-permute-start = (f32[16,16,128]{2,1,0:T(8,128)}, f32[16,16,128]{2,1,0:T(8,128)S(1)}, u32[]{:S(2)}, u32[]{:S(2)}) collective-permute-start(f32[16,16,128]{2,1,0:T(8,128)} %noisy_ref.1), channel_id=1, source_target_pairs={{4,8},{12,16},{20,24},{28,32},{36,40},{44,48},{52,56},{60,64},{68,... | collective-permute-start | bytes 393224 | tf_op jit(solution)/shard_map/ppermute | solution.py:452
  5.9 5.7 %collective-permute-start.1 = (f32[16,16,128]{2,1,0:T(8,128)}, f32[16,16,128]{2,1,0:T(8,128)S(1)}, u32[]{:S(2)}, u32[]{:S(2)}) collective-permute-start(f32[16,16,128]{2,1,0:T(8,128)} %noisy_ref.1), channel_id=1, source_target_pairs={{0,4},{8,12},{16,20},{24,28},{32,36},{40,44},{48,52},{56,60},{64,6... | collective-permute-start | bytes 393224 | tf_op jit(solution)/shard_map/ppermute | solution.py:452
  6.7 0.9 %copy-start = (f32[16,16,128]{2,1,0:T(8,128)S(1)}, f32[16,16,128]{2,1,0:T(8,128)}, u32[]{:S(2)}) copy-start(f32[16,16,128]{2,1,0:T(8,128)} %noisy_ref.1) | copy-start | bytes 393220
  15.7 6.5 %collective-permute-start.2 = (f32[3,8,128]{2,1,0:T(8,128)S(1)}, f32[3,8,128]{2,1,0:T(8,128)S(1)}, u32[]{:S(2)}, u32[]{:S(2)}) collective-permute-start(f32[3,8,128]{2,1,0:T(8,128)S(1)} %get-tuple-element.28), channel_id=1, source_target_pairs={{1,2},{2,1},{5,6},{6,5},{9,10},{10,9},{13,14},{14,13},{17,18},{18,... | collective-permute-start | bytes 36872 | tf_op jit(solution)/shard_map/ppermute | solution.py:452
  17.9 4.4 %collective-permute-start.3 = (f32[3,8,128]{2,1,0:T(8,128)S(1)}, f32[3,8,128]{2,1,0:T(8,128)S(1)}, u32[]{:S(2)}, u32[]{:S(2)}) collective-permute-start(f32[3,8,128]{2,1,0:T(8,128)S(1)} %get-tuple-element.29), channel_id=1, source_target_pairs={{0,1},{2,3},{1,0},{3,2},{4,5},{6,7},{5,4},{7,6},{8,9},{10,11},{9,8... | collective-permute-start | bytes 36872 | tf_op jit(solution)/shard_map/ppermute | solution.py:452

commit v6 on v5

--- a/solution.py
+++ b/solution.py
@@ -10,6 +10,7 @@
 F = jnp.float32
 B = jnp.bfloat16
 HALO = 4
+FIRST, REST = (4, 0), (1, 2, 3)
 SPLIT = 4
 
 
@@ -104,7 +105,7 @@
         parts.append(jnp.concatenate([high, (sums - high.astype(F)).astype(B)], 1))
 
 
-def accumulate(nx, segments, row, moved, below, rates, masks, column_mask, start, scratch):
+def accumulate(nx, segments, row, moved, below, rates, masks, column_mask, start, scratch, shifts=range(5)):
     kept, carry, weighted, totals = scratch
     last_slice = lax.broadcasted_iota(jnp.int32, (8, 128), 0) == 7
     carry_flat = carry.reshape(2 * nx * 4 * 16, 128)
@@ -116,7 +117,7 @@
     line = lax.broadcasted_iota(jnp.int32, (256, 128), 0) % 128
     column = lax.broadcasted_iota(jnp.int32, (256, 128), 1)
     band = jnp.where(abs(line - column) <= 2, 1.0, 0.0).astype(B)
-    for sy in range(5):
+    for sy in shifts:
         place = {}
         base, todo, parts = 0, [], []
         for shift_z in range(3):
@@ -276,7 +277,7 @@
 
 def join_kernel(
     next_ref, pair_ref, rim_ref, left_ref, right_ref, own_ref, copies, rate_ref, inner_w, inner_t,
-    low_ref, high_ref, rim_out, first_out, second_out, mid_ref, *scratch,
+    low_ref, high_ref, rim_out, first_out, second_out, sum_w, sum_t, *scratch,
 ):
     odd = flag("odd_x") > 0.5
     pair, other = pair_ref.reshape(256, 128), next_ref.reshape(256, 128)
@@ -313,26 +314,32 @@
 
     @pl.when(starts_early())
     def _():
-        outer_rows(own_ref, low_ref, high_ref, copies, rate_ref, inner_w, inner_t, mid_ref, *scratch)
+        outer_rows(own_ref, low_ref, high_ref, copies, rate_ref, inner_w, inner_t, FIRST, sum_w, sum_t, *scratch)
 
 
 def starts_early():
     return 2 * lax.axis_index("gy") < lax.axis_size("gy")
 
 
-def outer_kernel(own_ref, low_ref, high_ref, copies, rate_ref, inner_w, inner_t, done_ref, mid_ref, *scratch):
+def outer_kernel(own_ref, low_ref, high_ref, copies, rate_ref, inner_w, inner_t, done_w, done_t, mid_ref, sum_w, sum_t, *scratch):
     early = starts_early()
 
     @pl.when(early)
     def _():
-        mid_ref[...] = done_ref[...]
+        sum_w[...] = done_w[...]
+        sum_t[...] = done_t[...]
 
     @pl.when(jnp.logical_not(early))
     def _():
-        outer_rows(own_ref, low_ref, high_ref, copies, rate_ref, inner_w, inner_t, mid_ref, *scratch)
-
-
-def outer_rows(own_ref, low_ref, high_ref, copies, rate_ref, inner_w, inner_t, mid_ref, far, steps, below, *scratch):
+        outer_rows(own_ref, low_ref, high_ref, copies, rate_ref, inner_w, inner_t, FIRST, sum_w, sum_t, *scratch)
+
+    outer_rows(own_ref, low_ref, high_ref, copies, rate_ref, sum_w, sum_t, REST, sum_w, sum_t, *scratch)
+    for x in range(16):
+        for parity in range(2):
+            mid_ref[x, parity] = sum_w[x, parity] / sum_t[x, parity]
+
+
+def outer_rows(own_ref, low_ref, high_ref, copies, rate_ref, from_w, from_t, shifts, sum_w, sum_t, far, steps, below, *scratch):
     def row(x, parity):
         if x < 0:
             return low_ref[x + HALO, parity]
@@ -358,12 +365,10 @@
         (rate_ref[0], rate_ref[1]),
         (flag("below"), flag("above")),
         None,
-        lambda x, parity: (inner_w[x, parity], inner_t[x, parity]),
-        scratch,
+        lambda x, parity: (from_w[x, parity], from_t[x, parity]),
+        (*scratch, sum_w, sum_t),
+        shifts,
     )
-    for x in range(16):
-        for parity in range(2):
-            mid_ref[x, parity] = scratch[-2][x, parity] / scratch[-1][x, parity]
 
 
 def rim_kernel(rim_ref, second_ref, first_ref, rate_ref, mid_ref, out_ref, rows, copies, steps, below, column_mask, *scratch):
@@ -444,7 +449,7 @@
     )
 
 
-INPUTS = {"inner": 2, "join": 10, "outer": 8, "rim": 5}
+INPUTS = {"inner": 2, "join": 10, "outer": 9, "rim": 5}
 
 
 def swapped(value, axis, first):
@@ -469,15 +474,14 @@
     outer_scratch = (
         [V((5, 8, 5, 8, 128), F), V((8, 2, 16, 128), F), V((5, 20, 3, 8, 128), F)]
         + work(16, 18)
-        + [V((16, 2, 8, 128), F)] * 2
     )
-    low, high, rim, first, second, done = call(
-        join_kernel, "join", (row4, row4, row12, three, three, row16), outer_scratch, 20
+    low, high, rim, first, second, done_w, done_t = call(
+        join_kernel, "join", (row4, row4, row12, three, three, row16, row16), outer_scratch, 20
     )(other, pair, rim, to_left, to_right, own, copies, rate, inner_w, inner_t)
     second = swapped(second, "gy", 1)
     first = swapped(first, "gy", 0)
-    mid = call(outer_kernel, "outer", row16, outer_scratch, 20, 40_000_000)(
-        own, low, high, copies, rate, inner_w, inner_t, done
+    mid = call(outer_kernel, "outer", row16, [V((16, 2, 8, 128), F)] * 2 + outer_scratch, 20, 40_000_000)(
+        own, low, high, copies, rate, inner_w, inner_t, done_w, done_t
     )
     return call(
         rim_kernel,

time: 25.7 us -> 23.9 us (0.930)
  waiting for transfers between devices: 4.06 us -> 0.39 us
  starting transfers between devices: 8.24 us -> 10 us
    ppermute x4, waiting for transfers between devices: 4.06 us -> 0.39 us  [swapped(): return lax.ppermute(value, axis, pairs + [(b, a) for a, b in pairs])]
    ppermute x4, starting transfers between devices: 8.24 us -> 10 us  [swapped(): return lax.ppermute(value, axis, pairs + [(b, a) for a, b in pairs])]
  transfers between devices with their start and end apart: 4 -> 4, of which waited for: 1 -> 1; matrix products, arithmetic and copies ran while one was open for 3% -> 3% of each run, Pallas kernels for 17% -> 26%
where the time goes in v6:
time: 23.9 us; the launch traced here: 23.5 us
  Pallas kernels  11.5 us (48%)
  starting transfers between devices  10 us (42%)
  local copies, waits for them, and re-layouts  0.91 us (4%)
  other arithmetic  0.66 us (3%)
  waiting for transfers between devices  0.39 us (2%)
    ppermute x4, starting transfers between devices, swapped(): return lax.ppermute(value, axis, pairs + [(b, a) for a, b in pairs])  10 us
    pallas_call x1, Pallas kernels, per_device(): call(inner_kernel, 'inner', (row16, shape(2, 8, 128), shape(5, 16, 5, 8,...  4.05 us
    pallas_call x1, Pallas kernels, per_device(): call(rim_kernel, 'rim', shape(16, 16, 128), [V((12, 2, 8, 128), F), V((5,...  3.05 us
    pallas_call x1, Pallas kernels, per_device(): call(join_kernel, 'join', (row4, row4, row12, three, three, row16, row16)...  2.3 us
    pallas_call x1, Pallas kernels, per_device(): call(outer_kernel, 'outer', row16, [V((16, 2, 8, 128), F)] * 2 + outer_sc...  2.09 us
    unnamed x2, local copies, waits for them, and re-layouts  0.91 us
    reshape x1, other arithmetic, per_device(): rates = (-math.log2(math.e) / 125.0 / strength).reshape(1, 16)  0.66 us
  transfers between devices with their start and end apart: 4, of which 1 were waited for; matrix products, arithmetic and copies ran while one was open for 3% of the time, Pallas kernels for 26%

profile of v6, /device:TPU:25, one launch (start us, length us, event | category | flops | bytes accessed | tf_op | source)
XLA Modules:
  0.0 23.5 jit_solution(13200797208468377227)
XLA Ops:
  0.0 5.9 %collective-permute-start = (f32[16,16,128]{2,1,0:T(8,128)}, f32[16,16,128]{2,1,0:T(8,128)S(1)}, u32[]{:S(2)}, u32[]{:S(2)}) collective-permute-start(f32[16,16,128]{2,1,0:T(8,128)} %noisy_ref.1), channel_id=1, source_target_pairs={{4,8},{12,16},{20,24},{28,32},{36,40},{44,48},{52,56},{60,64},{68,... | collective-permute-start | bytes 393224 | tf_op jit(solution)/shard_map/ppermute | solution.py:457
  5.9 0.1 collective-permute-start.1
  6.0 0.7 %divide_bitcast_fusion.slices_ref = f32[1,16]{1,0:T(1,128)S(1)} fusion(f32[16]{0:T(128)} %param.3), kind=kLoop, calls=%fused_computation | loop fusion | flops 16 | bytes 128 | tf_op jit(solution)/shard_map/reshape | solution.py:463
  6.7 0.0 copy-start
  6.7 0.9 %copy-done = f32[16,16,128]{2,1,0:T(8,128)S(1)} copy-done((f32[16,16,128]{2,1,0:T(8,128)S(1)}, f32[16,16,128]{2,1,0:T(8,128)}, u32[]{:S(2)}) %copy-start) | copy-done | bytes 131096
  7.6 4.1 %inner.1 = (f32[16,2,8,128]{3,2,1,0:T(8,128)S(1)}, f32[2,8,128]{2,1,0:T(8,128)S(1)}, f32[5,16,5,8,128]{4,3,2,1,0:T(8,128)S(1)}, f32[16,2,8,128]{3,2,1,0:T(8,128)...) custom-call(f32[16,16,128]{2,1,0:T(8,128)S(1)} %copy-done, ...), custom_call_target="tpu_custom_call" | custom-call | flops 60000000 | bytes 500000 | tf_op jit(solution)/shard_map/inner/pallas_call | solution.py:466
  11.6 0.0 collective-permute-done.next_ref
  11.7 0.0 collective-permute-done.1.pair_ref
  11.7 2.3 %join.1 = (f32[4,2,8,128]{3,2,1,0:T(8,128)S(1)}, f32[4,2,8,128]{3,2,1,0:T(8,128)S(1)}, f32[12,2,8,128]{3,2,1,0:T(8,128)S(1)}, f32[3,8,128]{2,1,0:T(8,128)S(1)}, ...) custom-call(f32[16,16,128]{2,1,0:T(8,128)S(1)} %collective-permute-done.next_ref, ...), custom_call_target="tpu_custom_call" | custom-call | bytes 500000 | tf_op jit(solution)/shard_map/join/pallas_call | solution.py:478
  14.0 3.9 %collective-permute-start.2 = (f32[3,8,128]{2,1,0:T(8,128)S(1)}, f32[3,8,128]{2,1,0:T(8,128)S(1)}, u32[]{:S(2)}, u32[]{:S(2)}) collective-permute-start(f32[3,8,128]{2,1,0:T(8,128)S(1)} %get-tuple-element.29), channel_id=1, source_target_pairs={{1,2},{2,1},{5,6},{6,5},{9,10},{10,9},{13,14},{14,13},{17,18},{18,... | collective-permute-start | bytes 36872 | tf_op jit(solution)/shard_map/ppermute | solution.py:457
  17.9 0.1 collective-permute-start.3
  18.0 2.1 %outer.1.mid_ref = f32[16,2,8,128]{3,2,1,0:T(8,128)S(1)} custom-call(f32[16,2,8,128]{3,2,1,0:T(8,128)S(1)} %get-tuple-element.23.own_ref, f32[4,2,8,128]{3,2,1,0:T(8,128)S(1)} %get-tuple-element.31.low_ref, f32[4,2,8,128]{3,2,1,0:T(8,128)S(1)} %get-tuple-element.32.high_ref, f32[5,16,5,8,128]{4,3,2,1,0:T(8,128)S(1)} %get-tuple-element.24.copies, ...), custom_call_target="tpu_custom_call" | custom-call | flops 40000000 | bytes 500000 | tf_op jit(solution)/shard_map/outer/pallas_call | solution.py:483
  20.1 0.4 %collective-permute-done.2.second_ref = f32[3,8,128]{2,1,0:T(8,128)S(1)} collective-permute-done((f32[3,8,128]{2,1,0:T(8,128)S(1)}, f32[3,8,128]{2,1,0:T(8,128)S(1)}, u32[]{:S(2)}, u32[]{:S(2)}) %collective-permute-start.2) | collective-permute-done | bytes 12320 | tf_op jit(solution)/shard_map/ppermute | solution.py:457
  20.5 0.0 collective-permute-done.3.first_ref
  20.5 3.1 %rim.1 = f32[16,16,128]{2,1,0:T(8,128)} custom-call(f32[12,2,8,128]{3,2,1,0:T(8,128)S(1)} %get-tuple-element.28.rim_ref, f32[3,8,128]{2,1,0:T(8,128)S(1)} %collective-permute-done.2.second_ref, f32[3,8,128]{2,1,0:T(8,128)S(1)} %collective-permute-done.3.first_ref, f32[2,8,128]{2,1,0:T(8,128)S(1)} %get-tuple-element.25.rate_ref, ...), custom_call_target="tpu_custom_call" | custom-call | flops 20000000 | bytes 500000 | tf_op jit(solution)/shard_map/rim/pallas_call | solution.py:486
Async XLA Ops:
  0.0 11.6 %collective-permute-start = (f32[16,16,128]{2,1,0:T(8,128)}, f32[16,16,128]{2,1,0:T(8,128)S(1)}, u32[]{:S(2)}, u32[]{:S(2)}) collective-permute-start(f32[16,16,128]{2,1,0:T(8,128)} %noisy_ref.1), channel_id=1, source_target_pairs={{4,8},{12,16},{20,24},{28,32},{36,40},{44,48},{52,56},{60,64},{68,... | collective-permute-start | bytes 393224 | tf_op jit(solution)/shard_map/ppermute | solution.py:457
  5.9 5.7 %collective-permute-start.1 = (f32[16,16,128]{2,1,0:T(8,128)}, f32[16,16,128]{2,1,0:T(8,128)S(1)}, u32[]{:S(2)}, u32[]{:S(2)}) collective-permute-start(f32[16,16,128]{2,1,0:T(8,128)} %noisy_ref.1), channel_id=1, source_target_pairs={{0,4},{8,12},{16,20},{24,28},{32,36},{40,44},{48,52},{56,60},{64,6... | collective-permute-start | bytes 393224 | tf_op jit(solution)/shard_map/ppermute | solution.py:457
  6.7 0.9 %copy-start = (f32[16,16,128]{2,1,0:T(8,128)S(1)}, f32[16,16,128]{2,1,0:T(8,128)}, u32[]{:S(2)}) copy-start(f32[16,16,128]{2,1,0:T(8,128)} %noisy_ref.1) | copy-start | bytes 393220
  14.0 6.5 %collective-permute-start.2 = (f32[3,8,128]{2,1,0:T(8,128)S(1)}, f32[3,8,128]{2,1,0:T(8,128)S(1)}, u32[]{:S(2)}, u32[]{:S(2)}) collective-permute-start(f32[3,8,128]{2,1,0:T(8,128)S(1)} %get-tuple-element.29), channel_id=1, source_target_pairs={{1,2},{2,1},{5,6},{6,5},{9,10},{10,9},{13,14},{14,13},{17,18},{18,... | collective-permute-start | bytes 36872 | tf_op jit(solution)/shard_map/ppermute | solution.py:457
  17.9 2.6 %collective-permute-start.3 = (f32[3,8,128]{2,1,0:T(8,128)S(1)}, f32[3,8,128]{2,1,0:T(8,128)S(1)}, u32[]{:S(2)}, u32[]{:S(2)}) collective-permute-start(f32[3,8,128]{2,1,0:T(8,128)S(1)} %get-tuple-element.30), channel_id=1, source_target_pairs={{0,1},{2,3},{1,0},{3,2},{4,5},{6,7},{5,4},{7,6},{8,9},{10,11},{9,8... | collective-permute-start | bytes 36872 | tf_op jit(solution)/shard_map/ppermute | solution.py:457
